TPU v7x, 512 devices: a whole 4x4x16 slice. The times are simulated.
512 devices in a mesh: dp: 16 (over z), expert: 32 (over y, x, core).
Axes of the slice: x: 4, y: 4, z: 16, core: 2. Of those that a mesh axis runs over, the one named last changes fastest.
Arguments:
- tokens: bfloat16 [65536, 1024], P(('dp', 'expert')), may hold values from -6 to 6
- grad_out: bfloat16 [65536, 1024], P(('dp', 'expert')), may hold values from -6 to 6
- expert_ids: int32 [65536, 2], P(('dp', 'expert')), may hold values from 0 to 31, all different within a row; in each aligned block of 128 rows (0 to 127, 128 to 255, ...) at most 16 rows name the same one
- route_probs: bfloat16 [65536, 2], P(('dp', 'expert')), may hold values from 0.19921875 to 1
- gate_up_weight: bfloat16 [1024, 32, 1536], P('dp', 'expert'), may hold values from -0.1875 to 0.1875
- down_weight: bfloat16 [32, 768, 1024], P('expert'), may hold values from -0.21875 to 0.21875
- gate_up_scale_index: int32 [8, 32, 2], P(None, 'expert'), may hold values from 0 to 15
- down_scale_index: int32 [32, 6], P('expert'), may hold values from 0 to 15
- scale_table: float32 [16], replicated, may hold values from 0.5 to 2
Outputs:
- token_grad: bfloat16 [65536, 1024], P(('dp', 'expert'))
- prob_grad: float32 [65536, 2], P(('dp', 'expert'))
- gate_up_grad: bfloat16 [1024, 32, 1536], P('dp', 'expert')
- down_grad: bfloat16 [32, 768, 1024], P('expert')
Inputs may be any that keep to these rules, and one draw needn't show every extreme that they name: `expert_ids`: each row names two different experts. The 128 rows of one device name one expert at most 16 times, and in every draw some device's rows name some expert exactly 16 times.
All inputs are finite; a program needn't handle non-finite values.
Results may differ from a plain program's by a relative error of at most 0.022.
Values may be sent and summed in bfloat16 or wider, within the bound.
No kernel may reach another device: no remote copies, remote signals or barrier semaphores. Data moves between devices by JAX's collectives and lax.ppermute only.
A program may use at most 64 MiB of HBM per device.

v0:
```python
import jax
import jax.numpy as jnp
from jax import lax
from jax.sharding import PartitionSpec as P

QBLOCK = 128


def lookup(level_index, level_table):
    onehot = (level_index[..., None] == jnp.arange(level_table.shape[0], dtype=jnp.int32)).astype(
        level_table.dtype
    )
    return jnp.sum(onehot * level_table, axis=-1)


def slot_tables(routes, experts, capacity):
    flat_routes = routes.reshape(-1)
    expert_hits = (flat_routes[:, None] == jnp.arange(experts, dtype=jnp.int32)[None, :]).astype(
        jnp.int32
    )
    before = jnp.cumsum(expert_hits, axis=0) - expert_hits
    slot_rank = jnp.sum(before * expert_hits, axis=1)
    destination = flat_routes * capacity + slot_rank
    table_hits = destination[:, None] == jnp.arange(experts * capacity, dtype=jnp.int32)[None, :]
    return table_hits.astype(jnp.float32).reshape(routes.shape[0], 2, experts * capacity)


def body(
    tokens,
    grad_out,
    expert_ids,
    route_probs,
    gate_up_weight,
    down_weight,
    gate_up_scale_index,
    down_scale_index,
    scale_table,
):
    high = lax.Precision.HIGHEST
    f32 = jnp.float32
    groups = lax.axis_size("expert")
    tok_dev = tokens.shape[0]
    model_width = tokens.shape[1]
    per_device = down_weight.shape[0]
    hidden = down_weight.shape[1]
    experts = per_device * groups
    capacity = 4 * tok_dev // experts
    slots_all = experts * capacity
    slot_hits = slot_tables(expert_ids, experts, capacity)
    either = (slot_hits[:, 0] + slot_hits[:, 1]).astype(jnp.bfloat16)
    row_shape = (groups, per_device, capacity, model_width)
    send_tokens = (
        jnp.einsum("ts,td->sd", either, tokens, preferred_element_type=f32)
        .astype(jnp.bfloat16)
        .reshape(row_shape)
    )
    send_grads = (
        jnp.einsum("ts,td->sd", either, grad_out, preferred_element_type=f32)
        .astype(jnp.bfloat16)
        .reshape(row_shape)
    )
    send_probs = (
        jnp.einsum("tks,tk->s", slot_hits, route_probs.astype(f32), precision=high)
        .astype(jnp.bfloat16)
        .reshape(row_shape[:3])
    )
    recv_tokens, recv_grads, recv_probs = (
        lax.all_to_all(send_tokens, "expert", split_axis=0, concat_axis=0, tiled=True),
        lax.all_to_all(send_grads, "expert", split_axis=0, concat_axis=0, tiled=True),
        lax.all_to_all(send_probs, "expert", split_axis=0, concat_axis=0, tiled=True),
    )
    level_rows = jnp.repeat(lookup(gate_up_scale_index, scale_table), QBLOCK, axis=0)
    full_scale = jnp.repeat(level_rows, hidden, axis=2)
    down_scale = jnp.repeat(lookup(down_scale_index, scale_table), QBLOCK, axis=1)
    down_eff = (down_weight.astype(f32) * down_scale[:, :, None]).astype(jnp.bfloat16)
    gathered = lax.all_gather(gate_up_weight, "dp", axis=0, tiled=True)
    gate_up_eff = (gathered.astype(f32) * full_scale).astype(jnp.bfloat16)
    projected = jnp.einsum("sjcd,djf->sjcf", recv_tokens, gate_up_eff, preferred_element_type=f32)
    gate_part = projected[..., :hidden]
    up_part = projected[..., hidden:]
    sigmoid_gate = jax.nn.sigmoid(gate_part)
    activated = gate_part * sigmoid_gate
    hidden_rows = (activated * up_part).astype(jnp.bfloat16)
    hidden_grad = jnp.einsum("sjcd,jfd->sjcf", recv_grads, down_eff, preferred_element_type=f32)
    probs_wide = recv_probs.astype(f32)[..., None]
    scaled_grad = probs_wide * hidden_grad
    gate_grad = scaled_grad * up_part * sigmoid_gate * (1.0 + gate_part * (1.0 - sigmoid_gate))
    up_grad = scaled_grad * activated
    joint_grad = jnp.concatenate([gate_grad, up_grad], axis=-1).astype(jnp.bfloat16)
    row_grads = jnp.einsum(
        "sjcf,djf->sjcd", joint_grad, gate_up_eff, preferred_element_type=f32
    ).astype(jnp.bfloat16)
    back_rows = lax.all_to_all(row_grads, "expert", split_axis=0, concat_axis=0, tiled=True)
    token_grad = jnp.dot(
        either, back_rows.reshape(slots_all, model_width), preferred_element_type=f32
    ).astype(jnp.bfloat16)
    expert_out = jnp.einsum("sjcf,jfd->sjcd", hidden_rows, down_eff, preferred_element_type=f32)
    back_out = lax.all_to_all(
        expert_out.astype(jnp.bfloat16), "expert", split_axis=0, concat_axis=0, tiled=True
    ).astype(expert_out.dtype)
    picked = jnp.einsum(
        "tks,sd->tkd", slot_hits, back_out.reshape(slots_all, model_width), precision=high
    )
    prob_grad = jnp.sum(picked * grad_out.astype(f32)[:, None, :], axis=-1)
    weighted = (probs_wide * hidden_rows.astype(f32)).astype(jnp.bfloat16)
    partial_sum = jnp.einsum("sjcd,sjcf->djf", recv_tokens, joint_grad, preferred_element_type=f32)
    gate_up_grad = lax.psum_scatter(
        (partial_sum * full_scale).astype(jnp.bfloat16), "dp", scatter_dimension=0, tiled=True
    )
    down_part = (
        jnp.einsum("sjcf,sjcd->jfd", weighted, recv_grads, preferred_element_type=f32)
        * down_scale[:, :, None]
    )
    down_grad = lax.psum(down_part.astype(jnp.bfloat16), "dp")
    return (token_grad, prob_grad, gate_up_grad, down_grad)


def solution(mesh):
    in_specs = (
        P(("dp", "expert"), None),
        P(("dp", "expert"), None),
        P(("dp", "expert"), None),
        P(("dp", "expert"), None),
        P("dp", "expert", None),
        P("expert", None, None),
        P(None, "expert", None),
        P("expert", None),
        P(),
    )
    out_specs = (
        P(("dp", "expert"), None),
        P(("dp", "expert"), None),
        P("dp", "expert", None),
        P("expert", None, None),
    )
    return jax.shard_map(body, mesh=mesh, in_specs=in_specs, out_specs=out_specs, check_vma=False)
```

profile of v0, /device:TPU:6, one launch (start us, length us, event | category | flops | bytes accessed | tf_op | source)
XLA Modules:
  0.0 354.1 jit_solution(2820792020950934844)
XLA Ops:
  12.5 9.4 %all-to-all-start = ((bf16[32,1,16]{2,1,0:T(2,128)(2,1)}), bf16[32,1,16]{2,1,0:T(2,128)(2,1)S(1)}, u32[]{:S(2)}, u32[]{:S(2)}) async-start(bf16[32,1,16]{2,1,0:T(2,128)(2,1)} %reshape.263), calls=%async_computation | async-start | bytes 32768 | tf_op jit(solution)/shard_map/all_to_all | solution.py:70
  23.5 3.9 %all-to-all-done = bf16[32,1,16]{2,1,0:T(2,128)(2,1)S(1)} async-done(((bf16[32,1,16]{2,1,0:T(2,128)(2,1)}), bf16[32,1,16]{2,1,0:T(2,128)(2,1)S(1)}, u32[]{:S(2)}, u32[]{:S(2)}) %all-to-all-start) | async-done | bytes 1056 | tf_op jit(solution)/shard_map/all_to_all | solution.py:70
  27.4 6.3 %all-to-all-start.2 = ((bf16[32,1,16,1024]{3,2,1,0:T(8,128)(2,1)}), bf16[32,1,16,1024]{3,2,1,0:T(8,128)(2,1)}, u32[]{:S(2)}, u32[]{:S(2)}) async-start(bf16[32,1,16,1024]{3,2,1,0:T(8,128)(2,1)} %bitcast.20), calls=%async_computation.2 | async-start | bytes 2097152 | tf_op jit(solution)/shard_map/all_to_all | solution.py:68
  36.4 54.5 %all-gather.2.cloned.1.call-done = bf16[1024,1,1536]{2,0,1:T(8,128)(2,1)} async-done(((bf16[64,1,1536]{2,0,1:T(8,128)(2,1)}), bf16[1024,1,1536]{2,0,1:T(8,128)(2,1)}) %all-gather.2.cloned.1.call-update) | async-done | bytes 3145744 | tf_op jit(solution)/shard_map/all_gather | solution.py:76
  90.9 3.2 copy.84
  94.1 7.5 %all-to-all-start.1 = ((bf16[32,1,16,1024]{3,2,1,0:T(8,128)(2,1)}), bf16[32,1,16,1024]{3,2,1,0:T(8,128)(2,1)}, u32[]{:S(2)}, u32[]{:S(2)}) async-start(bf16[32,1,16,1024]{3,2,1,0:T(8,128)(2,1)} %bitcast.158), calls=%async_computation.1 | async-start | bytes 2097152 | tf_op jit(solution)/shard_map/all_to_all | solution.py:69
  103.8 1.7 copy-done.1
  105.5 1.7 copy-done.2
  107.2 5.1 %convolution_bitcast_fusion = f32[32,1,16,1536]{3,0,2,1:T(8,128)} fusion(bf16[1024,1536,1]{0,1,2:T(8,128)(2,1)S(1)} %fusion.3, bf16[32,1,16,1024]{3,2,1,0:T(8,128)(2,1)} %all-to-all-done.2), kind=kOutput, calls=%fused_computation.4 | convolution fusion | flops 1610612736 | bytes 7340032 | tf_op jit(solution)/shard_map/sjcd,djf->sjcf/dot_general | solution.py:78
  112.3 4.0 %all-to-all-done.1 = bf16[32,1,16,1024]{3,2,1,0:T(8,128)(2,1)} async-done(((bf16[32,1,16,1024]{3,2,1,0:T(8,128)(2,1)}), bf16[32,1,16,1024]{3,2,1,0:T(8,128)(2,1)}, u32[]{:S(2)}, u32[]{:S(2)}) %all-to-all-start.1) | async-done | bytes 1048608 | tf_op jit(solution)/shard_map/all_to_all | solution.py:69
  116.3 5.3 %fusion.29 = (bf16[32,16,768]{2,0,1:T(8,128)(2,1)S(1)}, bf16[32,16,768]{2,0,1:T(8,128)(2,1)S(1)}, bf16[32,1,16,768]{3,0,2,1:T(8,128)(2,1)}) fusion(f32[32,1,16,1536]{3,0,2,1:T(8,128)} %convolution_bitcast_fusion, bf16[32,1,16,1024]{3,2,1,0:T(8,128)(2,1)} %all-to-all-done.1, bf16[1,768,1024]{2,1,0:T(8,128)(2,1)S(1)} %copy-done.11, f32[768]{0:T(1024)S(1)} %copy-done.8, ...), kind=kOutput, calls=%fused_computation.46 | convolution fusion | flops 813957120 | bytes 8131584 | tf_op jit(solution)/shard_map/sjcd,jfd->sjcf/dot_general | solution.py:84
  121.6 3.8 %fusion.15 = f32[1536,1024,1]{1,0,2:T(8,128)S(1)} fusion(bf16[32,16,768]{2,0,1:T(8,128)(2,1)S(1)} %get-tuple-element.25, bf16[32,16,768]{2,0,1:T(8,128)(2,1)S(1)} %get-tuple-element.24, bf16[32,1,16,1024]{3,2,1,0:T(8,128)(2,1)} %all-to-all-done.2), kind=kOutput, calls=%fused_computation.33 | convolution fusion | flops 1613758464 | bytes 8912896 | tf_op jit(solution)/shard_map/sjcd,sjcf->djf/dot_general | solution.py:106
  125.5 1.8 fusion.2
  127.3 3.0 copy.104
  134.5 7.2 %all-to-all-start.4 = ((bf16[32,1,16,1024]{3,2,1,0:T(8,128)(2,1)}), bf16[32,1,16,1024]{3,2,1,0:T(8,128)(2,1)}, u32[]{:S(2)}, u32[]{:S(2)}) async-start(bf16[32,1,16,1024]{3,2,1,0:T(8,128)(2,1)} %copy.94), calls=%async_computation.4 | async-start | bytes 2097152 | tf_op jit(solution)/shard_map/all_to_all | solution.py:98
  142.0 4.1 %fusion.11 = bf16[1,768,1024]{2,1,0:T(8,128)(2,1)} fusion(f32[768]{0:T(1024)S(1)} %copy-done.8, bf16[32,1,16,1024]{3,2,1,0:T(8,128)(2,1)} %all-to-all-done.1, bf16[32,1,16,768]{3,0,2,1:T(8,128)(2,1)} %get-tuple-element.26, f32[32,16]{0,1:T(8,128)S(1)} %copy.86), kind=kOutput, calls=%fused_computation.23 | convolution fusion | flops 808058880 | bytes 3412992 | tf_op jit(solution)/shard_map/sjcf,sjcd->jfd/dot_general | solution.py:111
  146.1 3.2 fusion.13
  150.9 5.6 %all-to-all-done.4 = bf16[32,1,16,1024]{3,2,1,0:T(8,128)(2,1)} async-done(((bf16[32,1,16,1024]{3,2,1,0:T(8,128)(2,1)}), bf16[32,1,16,1024]{3,2,1,0:T(8,128)(2,1)}, u32[]{:S(2)}, u32[]{:S(2)}) %all-to-all-start.4) | async-done | bytes 1048608 | tf_op jit(solution)/shard_map/all_to_all | solution.py:98
  156.5 6.6 %all-to-all-start.3 = ((bf16[32,1,16,1024]{3,2,1,0:T(8,128)(2,1)}), bf16[32,1,16,1024]{3,2,1,0:T(8,128)(2,1)S(1)}, u32[]{:S(2)}, u32[]{:S(2)}) async-start(bf16[32,1,16,1024]{3,2,1,0:T(8,128)(2,1)} %copy.93), calls=%async_computation.3 | async-start | bytes 2097152 | tf_op jit(solution)/shard_map/all_to_all | solution.py:93
  163.1 2.4 fusion.14
  165.5 12.3 %all-to-all-done.3 = bf16[32,1,16,1024]{3,2,1,0:T(8,128)(2,1)S(1)} async-done(((bf16[32,1,16,1024]{3,2,1,0:T(8,128)(2,1)}), bf16[32,1,16,1024]{3,2,1,0:T(8,128)(2,1)S(1)}, u32[]{:S(2)}, u32[]{:S(2)}) %all-to-all-start.3) | async-done | bytes 1048608 | tf_op jit(solution)/shard_map/all_to_all | solution.py:93
  178.8 23.7 %reduce-scatter.4.cloned.1.call-done = bf16[64,1536]{1,0:T(8,128)(2,1)} async-done(((bf16[1024,1536]{1,0:T(8,128)(2,1)}), bf16[64,1536]{1,0:T(8,128)(2,1)}) %reduce-scatter.4.cloned.1.call-update) | async-done | bytes 196624
  204.4 140.5 %all-reduce.2.cloned.1.call-done = bf16[1,768,1024]{2,1,0:T(8,128)(2,1)} async-done(((bf16[1,768,1024]{2,1,0:T(8,128)(2,1)}), bf16[1,768,1024]{2,1,0:T(8,128)(2,1)}) %all-reduce.2.cloned.1.call-update) | async-done | bytes 1572880 | tf_op jit(solution)/shard_map/psum | solution.py:114
  344.9 2.7 copy.132
  (79 shorter events, 20.8 us)
Async XLA Ops:
  7.2 14.9 %copy-start = (bf16[128,1024]{1,0:T(8,128)(2,1)S(1)}, bf16[128,1024]{1,0:T(8,128)(2,1)}, u32[]{:S(2)}) copy-start(bf16[128,1024]{1,0:T(8,128)(2,1)} %param.9) | copy-start | bytes 786436
  7.2 83.7 %all-gather.2.cloned.1.call-start = ((), (), s32[]{:S(2)}) async-start(), calls=%async_computation.6 | async-start | bytes 3342336 | tf_op jit(solution)/shard_map/all_gather | solution.py:76
  10.8 11.0 %copy-start.6 = (s32[128,2]{0,1:T(2,128)}, s32[128,2]{0,1:T(2,128)S(1)}, u32[]{:S(2)}) copy-start(s32[128,2]{0,1:T(2,128)S(1)} %multiply_add_fusion) | copy-start | bytes 3076
  12.5 14.9 %all-to-all-start = ((bf16[32,1,16]{2,1,0:T(2,128)(2,1)}), bf16[32,1,16]{2,1,0:T(2,128)(2,1)S(1)}, u32[]{:S(2)}, u32[]{:S(2)}) async-start(bf16[32,1,16]{2,1,0:T(2,128)(2,1)} %reshape.263), calls=%async_computation | async-start | bytes 32768 | tf_op jit(solution)/shard_map/all_to_all | solution.py:70
  22.0 11.8 %copy-start.9 = (s32[8,1,2]{0,2,1:T(2,128)S(1)}, s32[8,1,2]{0,2,1:T(2,128)}, u32[]{:S(2)}) copy-start(s32[8,1,2]{0,2,1:T(2,128)} %param.15) | copy-start | bytes 196
  22.0 11.8 %copy-start.10 = (f32[16]{0:T(128)S(1)}, f32[16]{0:T(128)}, u32[]{:S(2)}) copy-start(f32[16]{0:T(128)} %param.17) | copy-start | bytes 196
  22.0 12.0 %copy-start.13 = (s32[1,6]{1,0:T(1,128)S(1)}, s32[1,6]{1,0:T(1,128)}, u32[]{:S(2)}) copy-start(s32[1,6]{1,0:T(1,128)} %param.16) | copy-start | bytes 76
  22.0 12.9 %copy-start.4 = (bf16[128,1024]{1,0:T(8,128)(2,1)S(1)}, bf16[128,1024]{1,0:T(8,128)(2,1)}, u32[]{:S(2)}) copy-start(bf16[128,1024]{1,0:T(8,128)(2,1)} %param.10) | copy-start | bytes 786436
  27.4 66.7 %all-to-all-start.2 = ((bf16[32,1,16,1024]{3,2,1,0:T(8,128)(2,1)}), bf16[32,1,16,1024]{3,2,1,0:T(8,128)(2,1)}, u32[]{:S(2)}, u32[]{:S(2)}) async-start(bf16[32,1,16,1024]{3,2,1,0:T(8,128)(2,1)} %bitcast.20), calls=%async_computation.2 | async-start | bytes 2097152 | tf_op jit(solution)/shard_map/all_to_all | solution.py:68
  94.1 22.2 %all-to-all-start.1 = ((bf16[32,1,16,1024]{3,2,1,0:T(8,128)(2,1)}), bf16[32,1,16,1024]{3,2,1,0:T(8,128)(2,1)}, u32[]{:S(2)}, u32[]{:S(2)}) async-start(bf16[32,1,16,1024]{3,2,1,0:T(8,128)(2,1)} %bitcast.158), calls=%async_computation.1 | async-start | bytes 2097152 | tf_op jit(solution)/shard_map/all_to_all | solution.py:69
  101.6 100.8 %reduce-scatter.4.cloned.1.call-start = ((), (), s32[]{:S(2)}) async-start(), calls=%async_computation.8 | async-start | bytes 3342336
  102.6 2.9 copy-start.1
  107.2 9.1 %copy-start.8 = (f32[768]{0:T(1024)S(1)}, f32[768]{0:T(1024)}, u32[]{:S(2)}) copy-start(f32[768]{0:T(1024)} %broadcast_bitcast_fusion.1) | copy-start | bytes 9220
  107.2 9.1 %copy-start.11 = (bf16[1,768,1024]{2,1,0:T(8,128)(2,1)S(1)}, bf16[1,768,1024]{2,1,0:T(8,128)(2,1)}, u32[]{:S(2)}) copy-start(bf16[1,768,1024]{2,1,0:T(8,128)(2,1)} %param.14) | copy-start | bytes 4718596
  116.3 9.2 %slice-start = ((s8[6291456]{0:T(1024)(128)(4,1)}), s8[4194304]{0:T(1024)(128)(4,1)S(1)}, s32[]{:S(2)}) async-start(s8[6291456]{0:T(1024)(128)(4,1)} %bitcast.155), calls=%async_computation.9 | async-start | bytes 8388608
  121.6 3.8 %copy-start.15 = (bf16[32,16,768]{2,0,1:T(8,128)(2,1)}, bf16[32,16,768]{2,0,1:T(8,128)(2,1)S(1)}, u32[]{:S(2)}) copy-start(bf16[32,16,768]{2,0,1:T(8,128)(2,1)S(1)} %get-tuple-element.24) | copy-start | bytes 2359300
  121.6 3.8 %copy-start.16 = (bf16[32,16,768]{2,0,1:T(8,128)(2,1)}, bf16[32,16,768]{2,0,1:T(8,128)(2,1)S(1)}, u32[]{:S(2)}) copy-start(bf16[32,16,768]{2,0,1:T(8,128)(2,1)S(1)} %get-tuple-element.25) | copy-start | bytes 2359300
  121.6 3.9 %slice-start.1 = ((s8[6291456]{0:T(1024)(128)(4,1)}), s8[2097152]{0:T(1024)(128)(4,1)S(1)}, s32[]{:S(2)}) async-start(s8[6291456]{0:T(1024)(128)(4,1)} %bitcast.155), calls=%async_computation.10 | async-start | bytes 4194304
  134.5 22.0 %all-to-all-start.4 = ((bf16[32,1,16,1024]{3,2,1,0:T(8,128)(2,1)}), bf16[32,1,16,1024]{3,2,1,0:T(8,128)(2,1)}, u32[]{:S(2)}, u32[]{:S(2)}) async-start(bf16[32,1,16,1024]{3,2,1,0:T(8,128)(2,1)} %copy.94), calls=%async_computation.4 | async-start | bytes 2097152 | tf_op jit(solution)/shard_map/all_to_all | solution.py:98
  141.7 4.4 %copy-start.3 = (bf16[1024,1536,1]{0,1,2:T(8,128)(2,1)S(1)}, bf16[1024,1536,1]{0,1,2:T(8,128)(2,1)}, u32[]{:S(2)}) copy-start(bf16[1024,1536,1]{0,1,2:T(8,128)(2,1)} %copy-done.2) | copy-start | bytes 9437188
  141.7 203.2 %all-reduce.2.cloned.1.call-start = ((), (), s32[]{:S(2)}) async-start(), calls=%async_computation.7 | async-start | bytes 3145728 | tf_op jit(solution)/shard_map/psum | solution.py:114
  149.3 13.8 %copy-start.5 = (bf16[128,1024]{1,0:T(8,128)(2,1)S(1)}, bf16[128,1024]{1,0:T(8,128)(2,1)}, u32[]{:S(2)}) copy-start(bf16[128,1024]{1,0:T(8,128)(2,1)} %param.10) | copy-start | bytes 786436
  149.3 13.8 %copy-start.7 = (s32[128,2]{0,1:T(2,128)S(1)}, s32[128,2]{0,1:T(2,128)}, u32[]{:S(2)}) copy-start(s32[128,2]{0,1:T(2,128)} %copy-done.6) | copy-start | bytes 3076
  156.5 21.3 %all-to-all-start.3 = ((bf16[32,1,16,1024]{3,2,1,0:T(8,128)(2,1)}), bf16[32,1,16,1024]{3,2,1,0:T(8,128)(2,1)S(1)}, u32[]{:S(2)}, u32[]{:S(2)}) async-start(bf16[32,1,16,1024]{3,2,1,0:T(8,128)(2,1)} %copy.93), calls=%async_computation.3 | async-start | bytes 2097152 | tf_op jit(solution)/shard_map/all_to_all | solution.py:93
  (3 other events, 4.7 us)
Sparse Core Ops, SparseCore 0:
  10.1 80.7 all-gather.1
  130.4 71.9 reduce-scatter.3
  205.3 139.5 all-reduce.1
where the time goes:
time: 355 us; the launch traced here: 354 us
  waiting for transfers between devices  245 us (69%)
  starting transfers between devices  37.5 us (11%)
  matrix products  29.7 us (8%)
  local copies, waits for them, and re-layouts  22.7 us (6%)
  between operations  14.1 us (4%)
  other arithmetic  4.95 us (1%)
    psum x1, waiting for transfers between devices, body(): down_grad = lax.psum(down_part.astype(jnp.bfloat16), 'dp')  141 us
    all_gather x1, waiting for transfers between devices, body(): gathered = lax.all_gather(gate_up_weight, 'dp', axis=0, tiled=True)  54.5 us
    unnamed x4, waiting for transfers between devices  24.4 us
    unnamed x45, local copies, waits for them, and re-layouts  13.5 us
    all_to_all x1, waiting for transfers between devices, body(): lax.all_to_all(row_grads, 'expert', split_axis=0, concat_axis=0, tiled=True)  12.3 us
    all_to_all x1, starting transfers between devices, body(): lax.all_to_all(send_probs, 'expert', split_axis=0, concat_axis=0, tiled=T...  9.37 us
    all_to_all x1, starting transfers between devices, body(): lax.all_to_all(send_grads, 'expert', split_axis=0, concat_axis=0, tiled=T...  7.5 us
    all_to_all x1, starting transfers between devices, body(): lax.all_to_all(expert_out.astype(jnp.bfloat16), 'expert', split_axis=0, c...  7.23 us
  transfers between devices with their start and end apart: 8, of which 7 were waited for; matrix products, arithmetic and copies ran while one was open for 10% of the time, Pallas kernels for 0%

commit v1 on v0

--- a/solution.py
+++ b/solution.py
@@ -18,7 +18,11 @@
     expert_hits = (flat_routes[:, None] == jnp.arange(experts, dtype=jnp.int32)[None, :]).astype(
         jnp.int32
     )
-    before = jnp.cumsum(expert_hits, axis=0) - expert_hits
+    place = jnp.arange(flat_routes.shape[0], dtype=jnp.int32)
+    earlier = (place[None, :] < place[:, None]).astype(jnp.bfloat16)
+    before = jnp.dot(
+        earlier, expert_hits.astype(jnp.bfloat16), preferred_element_type=jnp.float32
+    ).astype(jnp.int32)
     slot_rank = jnp.sum(before * expert_hits, axis=1)
     destination = flat_routes * capacity + slot_rank
     table_hits = destination[:, None] == jnp.arange(experts * capacity, dtype=jnp.int32)[None, :]

time: 355 us -> 355 us (level)
  no operation moved by 1% of the time
where the time goes in v1:
time: 355 us; the launch traced here: 354 us
  waiting for transfers between devices  246 us (69%)
  starting transfers between devices  37.2 us (10%)
  matrix products  30 us (8%)
  local copies, waits for them, and re-layouts  22.4 us (6%)
  between operations  14.1 us (4%)
  other arithmetic  4.22 us (1%)
    psum x1, waiting for transfers between devices, body(): down_grad = lax.psum(down_part.astype(jnp.bfloat16), 'dp')  140 us
    all_gather x1, waiting for transfers between devices, body(): gathered = lax.all_gather(gate_up_weight, 'dp', axis=0, tiled=True)  55.5 us
    unnamed x4, waiting for transfers between devices  24.6 us
    unnamed x45, local copies, waits for them, and re-layouts  13.5 us
    all_to_all x1, waiting for transfers between devices, body(): lax.all_to_all(row_grads, 'expert', split_axis=0, concat_axis=0, tiled=True)  12.3 us
    all_to_all x1, starting transfers between devices, body(): lax.all_to_all(send_probs, 'expert', split_axis=0, concat_axis=0, tiled=T...  9.37 us
    all_to_all x1, starting transfers between devices, body(): lax.all_to_all(send_grads, 'expert', split_axis=0, concat_axis=0, tiled=T...  7.22 us
    all_to_all x1, starting transfers between devices, body(): lax.all_to_all(expert_out.astype(jnp.bfloat16), 'expert', split_axis=0, c...  7.2 us
  transfers between devices with their start and end apart: 8, of which 7 were waited for; matrix products, arithmetic and copies ran while one was open for 10% of the time, Pallas kernels for 0%

profile of v1, /device:TPU:6, one launch (start us, length us, event | category | flops | bytes accessed | tf_op | source)
XLA Modules:
  0.0 353.9 jit_solution(2334480392853353179)
XLA Ops:
  11.6 9.4 %all-to-all-start = ((bf16[32,1,16]{2,1,0:T(2,128)(2,1)}), bf16[32,1,16]{2,1,0:T(2,128)(2,1)S(1)}, u32[]{:S(2)}, u32[]{:S(2)}) async-start(bf16[32,1,16]{2,1,0:T(2,128)(2,1)} %reshape.246), calls=%async_computation | async-start | bytes 32768 | tf_op jit(solution)/shard_map/all_to_all | solution.py:74
  22.6 3.9 %all-to-all-done = bf16[32,1,16]{2,1,0:T(2,128)(2,1)S(1)} async-done(((bf16[32,1,16]{2,1,0:T(2,128)(2,1)}), bf16[32,1,16]{2,1,0:T(2,128)(2,1)S(1)}, u32[]{:S(2)}, u32[]{:S(2)}) %all-to-all-start) | async-done | bytes 1056 | tf_op jit(solution)/shard_map/all_to_all | solution.py:74
  26.5 6.3 %all-to-all-start.2 = ((bf16[32,1,16,1024]{3,2,1,0:T(8,128)(2,1)}), bf16[32,1,16,1024]{3,2,1,0:T(8,128)(2,1)}, u32[]{:S(2)}, u32[]{:S(2)}) async-start(bf16[32,1,16,1024]{3,2,1,0:T(8,128)(2,1)} %bitcast.19), calls=%async_computation.2 | async-start | bytes 2097152 | tf_op jit(solution)/shard_map/all_to_all | solution.py:72
  35.5 55.5 %all-gather.2.cloned.1.call-done = bf16[1024,1,1536]{2,0,1:T(8,128)(2,1)} async-done(((bf16[64,1,1536]{2,0,1:T(8,128)(2,1)}), bf16[1024,1,1536]{2,0,1:T(8,128)(2,1)}) %all-gather.2.cloned.1.call-update) | async-done | bytes 3145744 | tf_op jit(solution)/shard_map/all_gather | solution.py:80
  91.0 3.2 copy.76
  94.2 7.2 %all-to-all-start.1 = ((bf16[32,1,16,1024]{3,2,1,0:T(8,128)(2,1)}), bf16[32,1,16,1024]{3,2,1,0:T(8,128)(2,1)}, u32[]{:S(2)}, u32[]{:S(2)}) async-start(bf16[32,1,16,1024]{3,2,1,0:T(8,128)(2,1)} %bitcast.139), calls=%async_computation.1 | async-start | bytes 2097152 | tf_op jit(solution)/shard_map/all_to_all | solution.py:73
  103.6 1.7 copy-done.1
  105.3 1.7 copy-done.2
  107.0 5.1 %convolution_bitcast_fusion = f32[32,1,16,1536]{3,0,2,1:T(8,128)} fusion(bf16[1024,1536,1]{0,1,2:T(8,128)(2,1)S(1)} %fusion.3, bf16[32,1,16,1024]{3,2,1,0:T(8,128)(2,1)} %all-to-all-done.2), kind=kOutput, calls=%fused_computation.4 | convolution fusion | flops 1610612736 | bytes 7340032 | tf_op jit(solution)/shard_map/sjcd,djf->sjcf/dot_general | solution.py:82
  112.1 4.0 %all-to-all-done.1 = bf16[32,1,16,1024]{3,2,1,0:T(8,128)(2,1)} async-done(((bf16[32,1,16,1024]{3,2,1,0:T(8,128)(2,1)}), bf16[32,1,16,1024]{3,2,1,0:T(8,128)(2,1)}, u32[]{:S(2)}, u32[]{:S(2)}) %all-to-all-start.1) | async-done | bytes 1048608 | tf_op jit(solution)/shard_map/all_to_all | solution.py:73
  116.1 5.3 %fusion.31 = (bf16[32,16,768]{2,0,1:T(8,128)(2,1)S(1)}, bf16[32,16,768]{2,0,1:T(8,128)(2,1)S(1)}, bf16[32,1,16,768]{3,0,2,1:T(8,128)(2,1)}) fusion(f32[32,1,16,1536]{3,0,2,1:T(8,128)} %convolution_bitcast_fusion, bf16[32,1,16,1024]{3,2,1,0:T(8,128)(2,1)} %all-to-all-done.1, bf16[1,768,1024]{2,1,0:T(8,128)(2,1)S(1)} %copy-done.11, f32[768]{0:T(1024)S(1)} %copy-done.8, ...), kind=kOutput, calls=%fused_computation.49 | convolution fusion | flops 813957120 | bytes 8131584 | tf_op jit(solution)/shard_map/sjcd,jfd->sjcf/dot_general | solution.py:88
  121.4 3.8 %fusion.17 = f32[1536,1024,1]{1,0,2:T(8,128)S(1)} fusion(bf16[32,16,768]{2,0,1:T(8,128)(2,1)S(1)} %get-tuple-element.25, bf16[32,16,768]{2,0,1:T(8,128)(2,1)S(1)} %get-tuple-element.24, bf16[32,1,16,1024]{3,2,1,0:T(8,128)(2,1)} %all-to-all-done.2), kind=kOutput, calls=%fused_computation.36 | convolution fusion | flops 1613758464 | bytes 8912896 | tf_op jit(solution)/shard_map/sjcd,sjcf->djf/dot_general | solution.py:110
  125.3 1.8 fusion.2
  127.1 3.0 copy.96
  134.3 7.2 %all-to-all-start.4 = ((bf16[32,1,16,1024]{3,2,1,0:T(8,128)(2,1)}), bf16[32,1,16,1024]{3,2,1,0:T(8,128)(2,1)}, u32[]{:S(2)}, u32[]{:S(2)}) async-start(bf16[32,1,16,1024]{3,2,1,0:T(8,128)(2,1)} %copy.86), calls=%async_computation.4 | async-start | bytes 2097152 | tf_op jit(solution)/shard_map/all_to_all | solution.py:102
  141.8 4.1 %fusion.11 = bf16[1,768,1024]{2,1,0:T(8,128)(2,1)} fusion(f32[768]{0:T(1024)S(1)} %copy-done.8, bf16[32,1,16,1024]{3,2,1,0:T(8,128)(2,1)} %all-to-all-done.1, bf16[32,1,16,768]{3,0,2,1:T(8,128)(2,1)} %get-tuple-element.26, f32[32,16]{0,1:T(8,128)S(1)} %copy.78), kind=kOutput, calls=%fused_computation.23 | convolution fusion | flops 808058880 | bytes 3412992 | tf_op jit(solution)/shard_map/sjcf,sjcd->jfd/dot_general | solution.py:115
  145.9 3.2 fusion.13
  150.7 5.6 %all-to-all-done.4 = bf16[32,1,16,1024]{3,2,1,0:T(8,128)(2,1)} async-done(((bf16[32,1,16,1024]{3,2,1,0:T(8,128)(2,1)}), bf16[32,1,16,1024]{3,2,1,0:T(8,128)(2,1)}, u32[]{:S(2)}, u32[]{:S(2)}) %all-to-all-start.4) | async-done | bytes 1048608 | tf_op jit(solution)/shard_map/all_to_all | solution.py:102
  156.3 6.6 %all-to-all-start.3 = ((bf16[32,1,16,1024]{3,2,1,0:T(8,128)(2,1)}), bf16[32,1,16,1024]{3,2,1,0:T(8,128)(2,1)S(1)}, u32[]{:S(2)}, u32[]{:S(2)}) async-start(bf16[32,1,16,1024]{3,2,1,0:T(8,128)(2,1)} %copy.85), calls=%async_computation.3 | async-start | bytes 2097152 | tf_op jit(solution)/shard_map/all_to_all | solution.py:97
  162.9 2.4 fusion.14
  165.3 12.3 %all-to-all-done.3 = bf16[32,1,16,1024]{3,2,1,0:T(8,128)(2,1)S(1)} async-done(((bf16[32,1,16,1024]{3,2,1,0:T(8,128)(2,1)}), bf16[32,1,16,1024]{3,2,1,0:T(8,128)(2,1)S(1)}, u32[]{:S(2)}, u32[]{:S(2)}) %all-to-all-start.3) | async-done | bytes 1048608 | tf_op jit(solution)/shard_map/all_to_all | solution.py:97
  178.6 23.9 %reduce-scatter.4.cloned.1.call-done = bf16[64,1536]{1,0:T(8,128)(2,1)} async-done(((bf16[1024,1536]{1,0:T(8,128)(2,1)}), bf16[64,1536]{1,0:T(8,128)(2,1)}) %reduce-scatter.4.cloned.1.call-update) | async-done | bytes 196624
  204.4 140.2 %all-reduce.2.cloned.1.call-done = bf16[1,768,1024]{2,1,0:T(8,128)(2,1)} async-done(((bf16[1,768,1024]{2,1,0:T(8,128)(2,1)}), bf16[1,768,1024]{2,1,0:T(8,128)(2,1)}) %all-reduce.2.cloned.1.call-update) | async-done | bytes 1572880 | tf_op jit(solution)/shard_map/psum | solution.py:118
  344.7 2.7 copy.122
  (73 shorter events, 20.0 us)
Async XLA Ops:
  7.2 14.0 %copy-start = (bf16[128,1024]{1,0:T(8,128)(2,1)S(1)}, bf16[128,1024]{1,0:T(8,128)(2,1)}, u32[]{:S(2)}) copy-start(bf16[128,1024]{1,0:T(8,128)(2,1)} %param.9) | copy-start | bytes 786436
  7.2 83.8 %all-gather.2.cloned.1.call-start = ((), (), s32[]{:S(2)}) async-start(), calls=%async_computation.6 | async-start | bytes 3342336 | tf_op jit(solution)/shard_map/all_gather | solution.py:80
  10.0 11.0 %copy-start.6 = (s32[128,2]{0,1:T(2,128)}, s32[128,2]{0,1:T(2,128)S(1)}, u32[]{:S(2)}) copy-start(s32[128,2]{0,1:T(2,128)S(1)} %multiply_add_fusion) | copy-start | bytes 3076
  11.6 14.9 %all-to-all-start = ((bf16[32,1,16]{2,1,0:T(2,128)(2,1)}), bf16[32,1,16]{2,1,0:T(2,128)(2,1)S(1)}, u32[]{:S(2)}, u32[]{:S(2)}) async-start(bf16[32,1,16]{2,1,0:T(2,128)(2,1)} %reshape.246), calls=%async_computation | async-start | bytes 32768 | tf_op jit(solution)/shard_map/all_to_all | solution.py:74
  21.1 11.8 %copy-start.9 = (s32[8,1,2]{0,2,1:T(2,128)S(1)}, s32[8,1,2]{0,2,1:T(2,128)}, u32[]{:S(2)}) copy-start(s32[8,1,2]{0,2,1:T(2,128)} %param.15) | copy-start | bytes 196
  21.1 11.8 %copy-start.10 = (f32[16]{0:T(128)S(1)}, f32[16]{0:T(128)}, u32[]{:S(2)}) copy-start(f32[16]{0:T(128)} %param.17) | copy-start | bytes 196
  21.1 12.0 %copy-start.13 = (s32[1,6]{1,0:T(1,128)S(1)}, s32[1,6]{1,0:T(1,128)}, u32[]{:S(2)}) copy-start(s32[1,6]{1,0:T(1,128)} %param.16) | copy-start | bytes 76
  21.1 12.9 %copy-start.4 = (bf16[128,1024]{1,0:T(8,128)(2,1)S(1)}, bf16[128,1024]{1,0:T(8,128)(2,1)}, u32[]{:S(2)}) copy-start(bf16[128,1024]{1,0:T(8,128)(2,1)} %param.10) | copy-start | bytes 786436
  26.5 67.7 %all-to-all-start.2 = ((bf16[32,1,16,1024]{3,2,1,0:T(8,128)(2,1)}), bf16[32,1,16,1024]{3,2,1,0:T(8,128)(2,1)}, u32[]{:S(2)}, u32[]{:S(2)}) async-start(bf16[32,1,16,1024]{3,2,1,0:T(8,128)(2,1)} %bitcast.19), calls=%async_computation.2 | async-start | bytes 2097152 | tf_op jit(solution)/shard_map/all_to_all | solution.py:72
  94.2 21.9 %all-to-all-start.1 = ((bf16[32,1,16,1024]{3,2,1,0:T(8,128)(2,1)}), bf16[32,1,16,1024]{3,2,1,0:T(8,128)(2,1)}, u32[]{:S(2)}, u32[]{:S(2)}) async-start(bf16[32,1,16,1024]{3,2,1,0:T(8,128)(2,1)} %bitcast.139), calls=%async_computation.1 | async-start | bytes 2097152 | tf_op jit(solution)/shard_map/all_to_all | solution.py:73
  101.4 101.0 %reduce-scatter.4.cloned.1.call-start = ((), (), s32[]{:S(2)}) async-start(), calls=%async_computation.8 | async-start | bytes 3342336
  102.4 2.9 copy-start.1
  107.0 9.1 %copy-start.8 = (f32[768]{0:T(1024)S(1)}, f32[768]{0:T(1024)}, u32[]{:S(2)}) copy-start(f32[768]{0:T(1024)} %broadcast_bitcast_fusion.1) | copy-start | bytes 9220
  107.0 9.1 %copy-start.11 = (bf16[1,768,1024]{2,1,0:T(8,128)(2,1)S(1)}, bf16[1,768,1024]{2,1,0:T(8,128)(2,1)}, u32[]{:S(2)}) copy-start(bf16[1,768,1024]{2,1,0:T(8,128)(2,1)} %param.14) | copy-start | bytes 4718596
  116.1 9.2 %slice-start = ((s8[6291456]{0:T(1024)(128)(4,1)}), s8[4194304]{0:T(1024)(128)(4,1)S(1)}, s32[]{:S(2)}) async-start(s8[6291456]{0:T(1024)(128)(4,1)} %bitcast.136), calls=%async_computation.9 | async-start | bytes 8388608
  121.4 3.8 %copy-start.15 = (bf16[32,16,768]{2,0,1:T(8,128)(2,1)}, bf16[32,16,768]{2,0,1:T(8,128)(2,1)S(1)}, u32[]{:S(2)}) copy-start(bf16[32,16,768]{2,0,1:T(8,128)(2,1)S(1)} %get-tuple-element.24) | copy-start | bytes 2359300
  121.4 3.8 %copy-start.16 = (bf16[32,16,768]{2,0,1:T(8,128)(2,1)}, bf16[32,16,768]{2,0,1:T(8,128)(2,1)S(1)}, u32[]{:S(2)}) copy-start(bf16[32,16,768]{2,0,1:T(8,128)(2,1)S(1)} %get-tuple-element.25) | copy-start | bytes 2359300
  121.4 3.9 %slice-start.1 = ((s8[6291456]{0:T(1024)(128)(4,1)}), s8[2097152]{0:T(1024)(128)(4,1)S(1)}, s32[]{:S(2)}) async-start(s8[6291456]{0:T(1024)(128)(4,1)} %bitcast.136), calls=%async_computation.10 | async-start | bytes 4194304
  134.3 22.0 %all-to-all-start.4 = ((bf16[32,1,16,1024]{3,2,1,0:T(8,128)(2,1)}), bf16[32,1,16,1024]{3,2,1,0:T(8,128)(2,1)}, u32[]{:S(2)}, u32[]{:S(2)}) async-start(bf16[32,1,16,1024]{3,2,1,0:T(8,128)(2,1)} %copy.86), calls=%async_computation.4 | async-start | bytes 2097152 | tf_op jit(solution)/shard_map/all_to_all | solution.py:102
  141.5 4.4 %copy-start.3 = (bf16[1024,1536,1]{0,1,2:T(8,128)(2,1)S(1)}, bf16[1024,1536,1]{0,1,2:T(8,128)(2,1)}, u32[]{:S(2)}) copy-start(bf16[1024,1536,1]{0,1,2:T(8,128)(2,1)} %copy-done.2) | copy-start | bytes 9437188
  141.5 203.1 %all-reduce.2.cloned.1.call-start = ((), (), s32[]{:S(2)}) async-start(), calls=%async_computation.7 | async-start | bytes 3145728 | tf_op jit(solution)/shard_map/psum | solution.py:118
  149.1 13.7 %copy-start.5 = (bf16[128,1024]{1,0:T(8,128)(2,1)S(1)}, bf16[128,1024]{1,0:T(8,128)(2,1)}, u32[]{:S(2)}) copy-start(bf16[128,1024]{1,0:T(8,128)(2,1)} %param.10) | copy-start | bytes 786436
  149.1 13.8 %copy-start.7 = (s32[128,2]{0,1:T(2,128)S(1)}, s32[128,2]{0,1:T(2,128)}, u32[]{:S(2)}) copy-start(s32[128,2]{0,1:T(2,128)} %copy-done.6) | copy-start | bytes 3076
  156.3 21.3 %all-to-all-start.3 = ((bf16[32,1,16,1024]{3,2,1,0:T(8,128)(2,1)}), bf16[32,1,16,1024]{3,2,1,0:T(8,128)(2,1)S(1)}, u32[]{:S(2)}, u32[]{:S(2)}) async-start(bf16[32,1,16,1024]{3,2,1,0:T(8,128)(2,1)} %copy.85), calls=%async_computation.3 | async-start | bytes 2097152 | tf_op jit(solution)/shard_map/all_to_all | solution.py:97
  (3 other events, 4.7 us)
Sparse Core Ops, SparseCore 0:
  10.1 80.8 all-gather.1
  130.2 72.1 reduce-scatter.3
  205.4 139.2 all-reduce.1

commit v2 on v0

v2 whole, which is shorter than its diff:
```python
import jax
import jax.numpy as jnp
from jax import lax
from jax.experimental import pallas as pl
from jax.experimental.pallas import tpu as pltpu
from jax.sharding import PartitionSpec as P

QBLOCK = 128
LANES = 128
FTILE = 256
bf16 = jnp.bfloat16
f32 = jnp.float32


def lookup(level_index, level_table):
    onehot = (level_index[..., None] == jnp.arange(level_table.shape[0], dtype=jnp.int32)).astype(
        level_table.dtype
    )
    return jnp.sum(onehot * level_table, axis=-1)


def slot_tables(routes, experts, capacity):
    flat_routes = routes.reshape(-1)
    expert_hits = (flat_routes[:, None] == jnp.arange(experts, dtype=jnp.int32)[None, :]).astype(
        jnp.int32
    )
    place = jnp.arange(flat_routes.shape[0], dtype=jnp.int32)
    earlier = (place[None, :] < place[:, None]).astype(bf16)
    before = jnp.dot(earlier, expert_hits.astype(bf16), preferred_element_type=f32).astype(
        jnp.int32
    )
    slot_rank = jnp.sum(before * expert_hits, axis=1)
    destination = flat_routes * capacity + slot_rank
    table_hits = destination[:, None] == jnp.arange(experts * capacity, dtype=jnp.int32)[None, :]
    return table_hits.astype(f32).reshape(routes.shape[0], 2, experts * capacity)


def scaled_rows(w_ref, scale_ref, part):
    blocks = w_ref.shape[0] // QBLOCK
    pieces = [
        (w_ref[QBLOCK * b : QBLOCK * (b + 1), :].astype(f32) * scale_ref[b, part]).astype(bf16)
        for b in range(blocks)
    ]
    return jnp.concatenate(pieces, axis=0)


def hidden_kernel(
    gu_scale, d_scale, x_ref, xt_ref, g_ref, hg_ref, wg_ref, wu_ref, sums_ref, joint_ref, dots_ref
):
    step = pl.program_id(0)
    x = x_ref[...]
    gate = jnp.dot(x, scaled_rows(wg_ref, gu_scale, 0), preferred_element_type=f32)
    up = jnp.dot(x, scaled_rows(wu_ref, gu_scale, 1), preferred_element_type=f32)
    sig = jax.nn.sigmoid(gate)
    act = gate * sig
    hidden = (act * up).astype(bf16)
    hg = hg_ref[...]
    joint = (
        (hg * up * sig * (1.0 + gate * (1.0 - sig))).astype(bf16),
        (hg * act).astype(bf16),
    )
    dots = jnp.sum(hidden.astype(f32) * hg, axis=1, keepdims=True)

    @pl.when(step == 0)
    def _():
        dots_ref[...] = dots

    @pl.when(step > 0)
    def _():
        dots_ref[...] += dots

    owners = sums_ref.shape[0]
    rows = xt_ref.shape[0] // owners
    xt = xt_ref[...]
    for k in range(2):
        joint_ref[k] = joint[k]
        part = jnp.dot(xt, joint[k], preferred_element_type=f32)
        for r in range(owners):
            piece = part[rows * r : rows * (r + 1), :] * gu_scale[rows * r // QBLOCK, k]
            for c in range(FTILE // LANES):
                at = (2 * k + c) * rows
                sums_ref[r, at : at + rows, :] = piece[:, LANES * c : LANES * (c + 1)].astype(bf16)
    part = lax.dot_general(
        hidden, g_ref[...], (((0,), (0,)), ((), ())), preferred_element_type=f32
    )
    drows = FTILE // owners
    base = 2 * (FTILE // LANES) * rows
    for r in range(owners):
        piece = part[drows * r : drows * (r + 1), :] * d_scale[
            step * (FTILE // QBLOCK) + drows * r // QBLOCK
        ]
        for c in range(part.shape[1] // LANES):
            at = base + c * drows
            sums_ref[r, at : at + drows, :] = piece[:, LANES * c : LANES * (c + 1)].astype(bf16)


def hidden_step(gu_scale, d_scale, x, xt, g, hg, weights, owners):
    slots, width = x.shape
    hidden = hg.shape[1]
    steps = hidden // FTILE
    rows = width // owners
    per_step = 2 * (FTILE // LANES) * rows + (FTILE // owners) * (width // LANES)
    smem = pl.BlockSpec(memory_space=pltpu.SMEM)
    whole = lambda a: pl.BlockSpec(a.shape, lambda i: (0, 0))
    flops = 2 * slots * width * hidden * 5
    return pl.pallas_call(
        hidden_kernel,
        grid=(steps,),
        in_specs=[
            smem,
            smem,
            whole(x),
            whole(xt),
            whole(g),
            pl.BlockSpec((slots, FTILE), lambda i: (0, i)),
            pl.BlockSpec((width, FTILE), lambda i: (0, i)),
            pl.BlockSpec((width, FTILE), lambda i, n=steps: (0, n + i)),
        ],
        out_specs=[
            pl.BlockSpec((owners, per_step, LANES), lambda i: (0, i, 0)),
            pl.BlockSpec((2, slots, FTILE), lambda i: (0, 0, i)),
            pl.BlockSpec((slots, 1), lambda i: (0, 0)),
        ],
        out_shape=[
            jax.ShapeDtypeStruct((owners, per_step * steps, LANES), bf16),
            jax.ShapeDtypeStruct((2, slots, hidden), bf16),
            jax.ShapeDtypeStruct((slots, 1), f32),
        ],
        compiler_params=pltpu.CompilerParams(vmem_limit_bytes=48 * 1024 * 1024),
        cost_estimate=pl.CostEstimate(
            flops=flops, bytes_accessed=14 * 1024 * 1024, transcendentals=slots * hidden
        ),
    )(gu_scale, d_scale, x, xt, g, hg, weights, weights)


def rows_kernel(gu_scale, joint_ref, wg_ref, wu_ref, out_ref, total):
    step = pl.program_id(0)
    contract = (((1,), (1,)), ((), ()))
    part = lax.dot_general(
        joint_ref[0], scaled_rows(wg_ref, gu_scale, 0), contract, preferred_element_type=f32
    ) + lax.dot_general(
        joint_ref[1], scaled_rows(wu_ref, gu_scale, 1), contract, preferred_element_type=f32
    )

    @pl.when(step == 0)
    def _():
        total[...] = part

    @pl.when(step > 0)
    def _():
        total[...] += part

    @pl.when(step == pl.num_programs(0) - 1)
    def _():
        out_ref[...] = total[...].astype(bf16)


def rows_step(gu_scale, joint, weights):
    slots, hidden = joint.shape[1:]
    width = weights.shape[0]
    steps = hidden // FTILE
    return pl.pallas_call(
        rows_kernel,
        grid=(steps,),
        in_specs=[
            pl.BlockSpec(memory_space=pltpu.SMEM),
            pl.BlockSpec((2, slots, FTILE), lambda i: (0, 0, i)),
            pl.BlockSpec((width, FTILE), lambda i: (0, i)),
            pl.BlockSpec((width, FTILE), lambda i, n=steps: (0, n + i)),
        ],
        out_specs=pl.BlockSpec((slots, width), lambda i: (0, 0)),
        out_shape=jax.ShapeDtypeStruct((slots, width), bf16),
        scratch_shapes=[pltpu.VMEM((slots, width), f32)],
        compiler_params=pltpu.CompilerParams(vmem_limit_bytes=32 * 1024 * 1024),
        cost_estimate=pl.CostEstimate(
            flops=4 * slots * width * hidden, bytes_accessed=6 * 1024 * 1024, transcendentals=0
        ),
    )(gu_scale, joint, weights, weights)


def body(
    tokens,
    grad_out,
    expert_ids,
    route_probs,
    gate_up_weight,
    down_weight,
    gate_up_scale_index,
    down_scale_index,
    scale_table,
):
    groups = lax.axis_size("expert")
    owners = lax.axis_size("dp")
    tok_dev, width = tokens.shape
    hidden = down_weight.shape[1]
    capacity = 4 * tok_dev // groups
    slots = groups * capacity
    steps = hidden // FTILE

    gathered = lax.all_gather(
        gate_up_weight.reshape(gate_up_weight.shape[0], 2 * hidden), "dp", axis=0, tiled=True
    )

    slot_hits = slot_tables(expert_ids, groups, capacity)
    either = (slot_hits[:, 0] + slot_hits[:, 1]).astype(bf16)
    weighing = jnp.sum(slot_hits * route_probs.astype(f32)[:, :, None], axis=1).astype(bf16)
    pack = lambda table, values: (
        jnp.einsum("ts,td->sd", table, values, preferred_element_type=f32)
        .astype(bf16)
        .reshape(groups, capacity, width)
    )
    send = jnp.concatenate([pack(either, tokens), pack(weighing, grad_out)], axis=1)
    recv = lax.all_to_all(send, "expert", split_axis=0, concat_axis=0, tiled=True)
    x = recv[:, :capacity].reshape(slots, width)
    g = recv[:, capacity:].reshape(slots, width)
    xt = x.T
    gu_scale = lookup(gate_up_scale_index[:, 0, :], scale_table)
    d_scale = lookup(down_scale_index[0], scale_table)
    down_eff = (
        down_weight[0].astype(f32) * jnp.repeat(d_scale, QBLOCK)[:, None]
    ).astype(bf16)
    hg = jnp.einsum("sd,fd->sf", g, down_eff, preferred_element_type=f32)

    sums, joint, dots = hidden_step(gu_scale, d_scale, x, xt, g, hg, gathered, owners)
    mine = lax.psum_scatter(sums, "dp", scatter_dimension=0, tiled=True)
    row_grads = rows_step(gu_scale, joint, gathered).reshape(groups, capacity, width)
    back_rows = lax.all_to_all(row_grads, "expert", split_axis=0, concat_axis=0, tiled=True)
    back_dots = lax.all_to_all(
        dots.reshape(groups, capacity), "expert", split_axis=0, concat_axis=0, tiled=True
    )
    token_grad = jnp.dot(
        either, back_rows.reshape(slots, width), preferred_element_type=f32
    ).astype(bf16)
    prob_grad = jnp.sum(slot_hits * back_dots.reshape(slots), axis=-1) / route_probs.astype(f32)

    rows = width // owners
    tiles = FTILE // LANES
    mine = mine.reshape(steps, -1, LANES)
    cut = 2 * tiles * rows
    gate_up_grad = (
        mine[:, :cut]
        .reshape(steps, 2, tiles, rows, LANES)
        .transpose(3, 1, 0, 2, 4)
        .reshape(rows, 1, 2 * hidden)
    )
    drows = FTILE // owners
    shared = lax.all_gather(
        mine[:, cut:].reshape(-1, LANES), "dp", axis=0, tiled=True
    ).reshape(owners, steps, width // LANES, drows, LANES)
    down_grad = shared.transpose(1, 0, 3, 2, 4).reshape(1, hidden, width)
    return (token_grad, prob_grad, gate_up_grad, down_grad)


def solution(mesh):
    in_specs = (
        P(("dp", "expert"), None),
        P(("dp", "expert"), None),
        P(("dp", "expert"), None),
        P(("dp", "expert"), None),
        P("dp", "expert", None),
        P("expert", None, None),
        P(None, "expert", None),
        P("expert", None),
        P(),
    )
    out_specs = (
        P(("dp", "expert"), None),
        P(("dp", "expert"), None),
        P("dp", "expert", None),
        P("expert", None, None),
    )
    return jax.shard_map(body, mesh=mesh, in_specs=in_specs, out_specs=out_specs, check_vma=False)
```

time: 355 us -> 263 us (0.74)
  waiting for transfers between devices: 245 us -> 183 us
  matrix products: 29.7 us -> 5.8 us
  Pallas kernels: 0 us -> 12.4 us
  starting transfers between devices: 37.5 us -> 25.1 us
  local copies, waits for them, and re-layouts: 22.7 us -> 15.4 us
    psum x1 -> x0, waiting for transfers between devices: 141 us -> none  [body(): down_grad = lax.psum(down_part.astype(jnp.bfloat16), 'dp')]
    reduce_scatter x0 -> x1, waiting for transfers between devices: none -> 78.2 us  [body(): mine = lax.psum_scatter(sums, 'dp', scatter_dimension=0, tiled=True)]
    dot_general x11 -> x5, matrix products: 29.7 us -> 5.8 us  [the longest x1 3.68 us: body(): hg = jnp.einsum('sd,fd->sf', g, down_eff, preferred_element_type=f32)]
    unnamed x4 -> x3, waiting for transfers between devices: 24.4 us -> 0.71 us
    all_to_all x4 -> x2, starting transfers between devices: 30.4 us -> 17.5 us  [the longest x1 10.4 us: body(): lax.all_to_all(send, 'expert', split_axis=0, concat_axis=0, tiled=True)]
    all_gather x1 -> x2, waiting for transfers between devices: 54.5 us -> 67.2 us  [the longest x1 35.1 us: body(): lax.all_gather(gate_up_weight.reshape(gate_up_weight.shape[0], 2 * hidden...]
    pallas_call x0 -> x2, Pallas kernels: none -> 12.4 us  [the longest x1 8.63 us: hidden_step(): pl.pallas_call(hidden_kernel, grid=(steps,), in_specs=[smem, smem, whole(...]
    all_to_all x4 -> x2, waiting for transfers between devices: 13.5 us -> 25.1 us  [the longest x1 25.1 us: body(): lax.all_to_all(send, 'expert', split_axis=0, concat_axis=0, tiled=True)]
  transfers between devices with their start and end apart: 8 -> 6, of which waited for: 7 -> 5; matrix products, arithmetic and copies ran while one was open for 10% -> 7% of each run, Pallas kernels for 0% -> 1%
where the time goes in v2:
time: 263 us; the launch traced here: 262 us
  waiting for transfers between devices  183 us (70%)
  starting transfers between devices  25.1 us (10%)
  local copies, waits for them, and re-layouts  15.4 us (6%)
  between operations  14 us (5%)
  Pallas kernels  12.4 us (5%)
  other arithmetic  6.78 us (3%)
  matrix products  5.8 us (2%)
    reduce_scatter x1, waiting for transfers between devices, body(): mine = lax.psum_scatter(sums, 'dp', scatter_dimension=0, tiled=True)  78.2 us
    all_gather x1, waiting for transfers between devices, body(): lax.all_gather(gate_up_weight.reshape(gate_up_weight.shape[0], 2 * hidden...  35.1 us
    all_gather x1, waiting for transfers between devices, body(): lax.all_gather(mine[:, cut:].reshape(-1, LANES), 'dp', axis=0, tiled=True)  32.1 us
    all_to_all x1, waiting for transfers between devices, body(): lax.all_to_all(send, 'expert', split_axis=0, concat_axis=0, tiled=True)  25.1 us
    all_to_all x1, waiting for transfers between devices, body(): lax.all_to_all(row_grads, 'expert', split_axis=0, concat_axis=0, tiled=True)  11.8 us
    all_to_all x1, starting transfers between devices, body(): lax.all_to_all(send, 'expert', split_axis=0, concat_axis=0, tiled=True)  10.4 us
    pallas_call x1, Pallas kernels, hidden_step(): pl.pallas_call(hidden_kernel, grid=(steps,), in_specs=[smem, smem, whole(...  8.63 us
    all_to_all x1, starting transfers between devices, body(): lax.all_to_all(row_grads, 'expert', split_axis=0, concat_axis=0, tiled=True)  7.52 us
  transfers between devices with their start and end apart: 6, of which 5 were waited for; matrix products, arithmetic and copies ran while one was open for 7% of the time, Pallas kernels for 1%

profile of v2, /device:TPU:6, one launch (start us, length us, event | category | flops | bytes accessed | tf_op | source)
XLA Modules:
  0.0 262.5 jit_solution(2558030401318256183)
XLA Ops:
  7.9 0.8 copy.53
  11.9 1.5 pad_maximum_fusion
  13.4 10.4 %all-to-all-start = ((bf16[32,32,1024]{2,1,0:T(8,128)(2,1)}), bf16[32,32,1024]{2,1,0:T(8,128)(2,1)}, u32[]{:S(2)}, u32[]{:S(2)}) async-start(bf16[32,32,1024]{2,1,0:T(8,128)(2,1)} %pad_maximum_fusion), calls=%async_computation | async-start | bytes 4194304 | tf_op jit(solution)/shard_map/all_to_all | solution.py:213
  24.3 25.1 %all-to-all-done = bf16[32,32,1024]{2,1,0:T(8,128)(2,1)} async-done(((bf16[32,32,1024]{2,1,0:T(8,128)(2,1)}), bf16[32,32,1024]{2,1,0:T(8,128)(2,1)}, u32[]{:S(2)}, u32[]{:S(2)}) %all-to-all-start) | async-done | bytes 2097184 | tf_op jit(solution)/shard_map/all_to_all | solution.py:213
  49.4 1.7 fusion.11
  51.7 3.7 %fusion.1.hg_ref = f32[512,768]{1,0:T(8,128)} fusion(bf16[512,1024]{1,0:T(8,128)(2,1)S(1)} %bitcast.44, bf16[1,768,1024]{2,1,0:T(8,128)(2,1)} %param.14, f32[768]{0:T(1024)S(1)} %broadcast_bitcast_fusion), kind=kOutput, calls=%fused_computation.3 | convolution fusion | flops 807665664 | bytes 4197376 | tf_op jit(solution)/shard_map/sd,fd->sf/dot_general | solution.py:222
  55.4 35.1 %all-gather.6.cloned.1.call-done = bf16[1024,1,1536]{2,0,1:T(8,128)(2,1)} async-done(((bf16[64,1,1536]{2,0,1:T(8,128)(2,1)}), bf16[1024,1,1536]{2,0,1:T(8,128)(2,1)}) %all-gather.6.cloned.1.call-update) | async-done | bytes 3145744 | tf_op jit(solution)/shard_map/all_gather | solution.py:200
  90.5 8.6 %shard_map.120 = (bf16[16,1152,128]{2,1,0:T(8,128)(2,1)}, bf16[2,512,768]{2,1,0:T(8,128)(2,1)S(1)}, f32[512,1]{1,0:T(8,128)S(1)}) custom-call(f32[8,2]{1,0:T(8,128)S(1)} %copy.57.gu_scale, f32[6]{0:T(128)S(1)} %select_reduce_fusion.3.d_scale, bf16[512,1024]{1,0:T(8,128)(2,1)S(1)} %bitcast.41, bf16[1024,512]{1,0:T(8,128)(2,1)S(1)} %bitcast.43, ...), custom_call_target="tpu_custom_call" | custom-call | flops 4026531840 | bytes 14680064 | tf_op jit(solution)/shard_map/pallas_call | solution.py:106
  99.1 1.1 copy-done.3
  101.0 78.2 %reduce-scatter.2.cloned.1.call-done = bf16[1,1152,128]{2,1,0:T(8,128)(2,1)} async-done(((bf16[16,1152,128]{2,1,0:T(8,128)(2,1)}), bf16[1,1152,128]{2,1,0:T(8,128)(2,1)}) %reduce-scatter.2.cloned.1.call-update) | async-done | bytes 294928 | tf_op jit(solution)/shard_map/reduce_scatter | solution.py:225
  179.2 1.5 slice.29
  180.8 1.1 reduce
  182.6 7.1 %all-to-all-start.2 = ((f32[32,1,16]{2,1,0:T(1,128)}), f32[32,1,16]{2,1,0:T(1,128)}, u32[]{:S(2)}, u32[]{:S(2)}) async-start(f32[32,1,16]{2,1,0:T(1,128)} %bitcast.55), calls=%async_computation.2 | async-start | bytes 32768 | tf_op jit(solution)/shard_map/all_to_all | solution.py:228
  189.7 1.4 copy-done.4
  191.1 3.7 %shard_map.121 = bf16[512,1024]{1,0:T(8,128)(2,1)S(1)} custom-call(f32[8,2]{1,0:T(8,128)S(1)} %copy.57.gu_scale, bf16[2,512,768]{2,1,0:T(8,128)(2,1)S(1)} %copy-done.4, bf16[1024,1536]{1,0:T(8,128)(2,1)S(1)} %bitcast.38, bf16[1024,1536]{1,0:T(8,128)(2,1)S(1)} %bitcast.39), custom_call_target="tpu_custom_call" | custom-call | flops 1610612736 | bytes 6291456 | tf_op jit(solution)/shard_map/pallas_call | solution.py:162
  194.9 1.0 copy-done.2
  195.8 7.5 %all-to-all-start.1 = ((bf16[32,16,1024]{2,1,0:T(8,128)(2,1)}), bf16[32,16,1024]{2,1,0:T(8,128)(2,1)S(1)}, u32[]{:S(2)}, u32[]{:S(2)}) async-start(bf16[32,16,1024]{2,1,0:T(8,128)(2,1)} %bitcast.42), calls=%async_computation.1 | async-start | bytes 2097152 | tf_op jit(solution)/shard_map/all_to_all | solution.py:227
  203.9 1.4 reduce.4
  206.2 11.8 %all-to-all-done.1 = bf16[32,16,1024]{2,1,0:T(8,128)(2,1)S(1)} async-done(((bf16[32,16,1024]{2,1,0:T(8,128)(2,1)}), bf16[32,16,1024]{2,1,0:T(8,128)(2,1)S(1)}, u32[]{:S(2)}, u32[]{:S(2)}) %all-to-all-start.1) | async-done | bytes 1048608 | tf_op jit(solution)/shard_map/all_to_all | solution.py:227
  218.0 1.0 convolution_convert_fusion.2
  219.2 0.8 reshape.98
  220.0 32.1 %all-gather.4.cloned.1.call-done = bf16[6144,128]{1,0:T(8,128)(2,1)} async-done(((bf16[384,128]{1,0:T(8,128)(2,1)}), bf16[6144,128]{1,0:T(8,128)(2,1)}) %all-gather.4.cloned.1.call-update) | async-done | bytes 1572880 | tf_op jit(solution)/shard_map/all_gather | solution.py:247
  252.1 1.8 copy.60
  253.9 2.1 reshape.101
  (51 shorter events, 8.0 us)
Async XLA Ops:
  7.2 3.8 %copy-start = (bf16[128,1024]{1,0:T(8,128)(2,1)S(1)}, bf16[128,1024]{1,0:T(8,128)(2,1)}, u32[]{:S(2)}) copy-start(bf16[128,1024]{1,0:T(8,128)(2,1)} %param.9) | copy-start | bytes 786436
  7.2 4.2 %copy-start.7 = (bf16[128,1024]{1,0:T(8,128)(2,1)S(1)}, bf16[128,1024]{1,0:T(8,128)(2,1)}, u32[]{:S(2)}) copy-start(bf16[128,1024]{1,0:T(8,128)(2,1)} %param.10) | copy-start | bytes 786436
  7.2 83.3 %all-gather.6.cloned.1.call-start = ((), (), s32[]{:S(2)}) async-start(), calls=%async_computation.6 | async-start | bytes 3342336 | tf_op jit(solution)/shard_map/all_gather | solution.py:200
  13.4 10.4 %copy-start.8 = (s32[8,1,2]{0,2,1:T(2,128)S(1)}, s32[8,1,2]{0,2,1:T(2,128)}, u32[]{:S(2)}) copy-start(s32[8,1,2]{0,2,1:T(2,128)} %param.15) | copy-start | bytes 196
  13.4 10.4 %copy-start.9 = (f32[16]{0:T(128)S(1)}, f32[16]{0:T(128)}, u32[]{:S(2)}) copy-start(f32[16]{0:T(128)} %param.17) | copy-start | bytes 196
  13.4 10.7 %copy-start.11 = (s32[1,6]{1,0:T(1,128)S(1)}, s32[1,6]{1,0:T(1,128)}, u32[]{:S(2)}) copy-start(s32[1,6]{1,0:T(1,128)} %param.16) | copy-start | bytes 76
  13.4 36.0 %all-to-all-start = ((bf16[32,32,1024]{2,1,0:T(8,128)(2,1)}), bf16[32,32,1024]{2,1,0:T(8,128)(2,1)}, u32[]{:S(2)}, u32[]{:S(2)}) async-start(bf16[32,32,1024]{2,1,0:T(8,128)(2,1)} %pad_maximum_fusion), calls=%async_computation | async-start | bytes 4194304 | tf_op jit(solution)/shard_map/all_to_all | solution.py:213
  23.8 155.5 %reduce-scatter.2.cloned.1.call-start = ((), (), s32[]{:S(2)}) async-start(), calls=%async_computation.4 | async-start | bytes 5013504 | tf_op jit(solution)/shard_map/reduce_scatter | solution.py:225
  99.1 1.1 copy-start.3
  100.2 0.7 copy-start.5
  100.9 88.8 %copy-start.1 = (bf16[1024,1,1536]{2,0,1:T(8,128)(2,1)S(1)}, bf16[1024,1,1536]{2,0,1:T(8,128)(2,1)}, u32[]{:S(2)}) copy-start(bf16[1024,1,1536]{2,0,1:T(8,128)(2,1)} %all-gather.6.cloned.1.call-done) | copy-start | bytes 9437188
  101.0 151.1 %all-gather.4.cloned.1.call-start = ((), (), s32[]{:S(2)}) async-start(), calls=%async_computation.5 | async-start | bytes 1671168 | tf_op jit(solution)/shard_map/all_gather | solution.py:247
  182.6 13.3 %all-to-all-start.2 = ((f32[32,1,16]{2,1,0:T(1,128)}), f32[32,1,16]{2,1,0:T(1,128)}, u32[]{:S(2)}, u32[]{:S(2)}) async-start(f32[32,1,16]{2,1,0:T(1,128)} %bitcast.55), calls=%async_computation.2 | async-start | bytes 32768 | tf_op jit(solution)/shard_map/all_to_all | solution.py:228
  189.7 1.4 copy-start.4
  194.9 1.0 copy-start.2
  195.8 9.7 %copy-start.10 = (bf16[128,2]{0,1:T(2,128)(2,1)S(1)}, bf16[128,2]{0,1:T(2,128)(2,1)}, u32[]{:S(2)}) copy-start(bf16[128,2]{0,1:T(2,128)(2,1)} %param.12) | copy-start | bytes 1540
  195.8 23.2 %copy-start.6 = (bf16[1,1152,128]{2,1,0:T(8,128)(2,1)S(1)}, bf16[1,1152,128]{2,1,0:T(8,128)(2,1)}, u32[]{:S(2)}) copy-start(bf16[1,1152,128]{2,1,0:T(8,128)(2,1)} %reduce-scatter.2.cloned.1.call-done) | copy-start | bytes 884740
  195.8 22.2 %all-to-all-start.1 = ((bf16[32,16,1024]{2,1,0:T(8,128)(2,1)}), bf16[32,16,1024]{2,1,0:T(8,128)(2,1)S(1)}, u32[]{:S(2)}, u32[]{:S(2)}) async-start(bf16[32,16,1024]{2,1,0:T(8,128)(2,1)} %bitcast.42), calls=%async_computation.1 | async-start | bytes 2097152 | tf_op jit(solution)/shard_map/all_to_all | solution.py:227
Sparse Core Ops, SparseCore 0:
  10.1 80.3 all-gather.5
  101.1 78.0 reduce-scatter.1
  181.3 70.7 all-gather.3

commit v3 on v2

--- a/solution.py
+++ b/solution.py
@@ -86,8 +86,9 @@
     drows = FTILE // owners
     base = 2 * (FTILE // LANES) * rows
     for r in range(owners):
-        piece = part[drows * r : drows * (r + 1), :] * d_scale[
-            step * (FTILE // QBLOCK) + drows * r // QBLOCK
+        own = (r % 2) * (owners // 2) + r // 2
+        piece = part[drows * own : drows * (own + 1), :] * d_scale[
+            step * (FTILE // QBLOCK) + drows * own // QBLOCK
         ]
         for c in range(part.shape[1] // LANES):
             at = base + c * drows
@@ -233,6 +234,7 @@
     ).astype(bf16)
     prob_grad = jnp.sum(slot_hits * back_dots.reshape(slots), axis=-1) / route_probs.astype(f32)
 
+    mine, token_grad, prob_grad = lax.optimization_barrier((mine, token_grad, prob_grad))
     rows = width // owners
     tiles = FTILE // LANES
     mine = mine.reshape(steps, -1, LANES)
@@ -244,10 +246,22 @@
         .reshape(rows, 1, 2 * hidden)
     )
     drows = FTILE // owners
-    shared = lax.all_gather(
-        mine[:, cut:].reshape(-1, LANES), "dp", axis=0, tiled=True
-    ).reshape(owners, steps, width // LANES, drows, LANES)
-    down_grad = shared.transpose(1, 0, 3, 2, 4).reshape(1, hidden, width)
+    own = (
+        mine[:, cut:]
+        .reshape(steps, width // LANES, drows, LANES)
+        .transpose(0, 2, 1, 3)
+        .reshape(steps, drows, width)
+    )
+    same_parity = [list(range(k, owners, 2)) for k in range(2)]
+    neighbours = [[k, k + 1] for k in range(0, owners, 2)]
+    gather = lambda a, sets: lax.all_gather(
+        a, "dp", axis=1, tiled=True, axis_index_groups=sets
+    )
+    half = gather(own, same_parity)
+    down_grad = jnp.concatenate(
+        [gather(half[:, :, : width // 2], neighbours), gather(half[:, :, width // 2 :], neighbours)],
+        axis=2,
+    ).reshape(1, hidden, width)
     return (token_grad, prob_grad, gate_up_grad, down_grad)
 
 

time: 263 us -> 242 us (0.920)
  waiting for transfers between devices: 183 us -> 113 us
  blocking collectives: 0 us -> 49.4 us
  local copies, waits for them, and re-layouts: 15.4 us -> 12 us
    all_gather x0 -> x3, blocking collectives: none -> 49.4 us  [body(): lax.all_gather(a, 'dp', axis=1, tiled=True, axis_index_groups=sets)]
    reduce_scatter x1, waiting for transfers between devices: 78.2 us -> 40.2 us  [body(): mine = lax.psum_scatter(sums, 'dp', scatter_dimension=0, tiled=True)]
    all_gather x1 -> x0, waiting for transfers between devices: 32.1 us -> none  [body(): lax.all_gather(mine[:, cut:].reshape(-1, LANES), 'dp', axis=0, tiled=True)]
  transfers between devices with their start and end apart: 6 -> 5, of which waited for: 5 -> 4; matrix products, arithmetic and copies ran while one was open for 7% -> 7% of each run, Pallas kernels for 1% -> 2%
where the time goes in v3:
time: 242 us; the launch traced here: 241 us
  waiting for transfers between devices  113 us (47%)
  blocking collectives  49.4 us (20%)
  starting transfers between devices  25.5 us (11%)
  between operations  14.3 us (6%)
  Pallas kernels  12.3 us (5%)
  local copies, waits for them, and re-layouts  12 us (5%)
  other arithmetic  8.32 us (3%)
  matrix products  5.82 us (2%)
    all_gather x3, blocking collectives, body(): lax.all_gather(a, 'dp', axis=1, tiled=True, axis_index_groups=sets)  49.4 us
    reduce_scatter x1, waiting for transfers between devices, body(): mine = lax.psum_scatter(sums, 'dp', scatter_dimension=0, tiled=True)  40.2 us
    all_gather x1, waiting for transfers between devices, body(): lax.all_gather(gate_up_weight.reshape(gate_up_weight.shape[0], 2 * hidden...  35.1 us
    all_to_all x1, waiting for transfers between devices, body(): lax.all_to_all(send, 'expert', split_axis=0, concat_axis=0, tiled=True)  25.1 us
    all_to_all x1, waiting for transfers between devices, body(): lax.all_to_all(row_grads, 'expert', split_axis=0, concat_axis=0, tiled=True)  11.8 us
    all_to_all x1, starting transfers between devices, body(): lax.all_to_all(send, 'expert', split_axis=0, concat_axis=0, tiled=True)  10.4 us
    pallas_call x1, Pallas kernels, hidden_step(): pl.pallas_call(hidden_kernel, grid=(steps,), in_specs=[smem, smem, whole(...  8.61 us
    all_to_all x1, starting transfers between devices, body(): lax.all_to_all(dots.reshape(groups, capacity), 'expert', split_axis=0, co...  7.6 us
  transfers between devices with their start and end apart: 5, of which 4 were waited for; matrix products, arithmetic and copies ran while one was open for 7% of the time, Pallas kernels for 2%

profile of v3, /device:TPU:6, one launch (start us, length us, event | category | flops | bytes accessed | tf_op | source)
XLA Modules:
  0.0 240.6 jit_solution(7136521188551560657)
XLA Ops:
  11.9 1.5 pad_maximum_fusion
  13.4 10.4 %all-to-all-start = ((bf16[32,32,1024]{2,1,0:T(8,128)(2,1)}), bf16[32,32,1024]{2,1,0:T(8,128)(2,1)}, u32[]{:S(2)}, u32[]{:S(2)}) async-start(bf16[32,32,1024]{2,1,0:T(8,128)(2,1)} %pad_maximum_fusion), calls=%async_computation | async-start | bytes 4194304 | tf_op jit(solution)/shard_map/all_to_all | solution.py:214
  24.3 25.1 %all-to-all-done = bf16[32,32,1024]{2,1,0:T(8,128)(2,1)} async-done(((bf16[32,32,1024]{2,1,0:T(8,128)(2,1)}), bf16[32,32,1024]{2,1,0:T(8,128)(2,1)}, u32[]{:S(2)}, u32[]{:S(2)}) %all-to-all-start) | async-done | bytes 2097184 | tf_op jit(solution)/shard_map/all_to_all | solution.py:214
  49.5 1.7 fusion.11
  51.7 3.7 %fusion.1.hg_ref = f32[512,768]{1,0:T(8,128)} fusion(bf16[512,1024]{1,0:T(8,128)(2,1)S(1)} %bitcast.46, bf16[1,768,1024]{2,1,0:T(8,128)(2,1)} %param.14, f32[768]{0:T(1024)S(1)} %broadcast_bitcast_fusion), kind=kOutput, calls=%fused_computation.3 | convolution fusion | flops 807665664 | bytes 4197376 | tf_op jit(solution)/shard_map/sd,fd->sf/dot_general | solution.py:223
  55.4 35.1 %all-gather.3.cloned.1.call-done = bf16[1024,1,1536]{2,0,1:T(8,128)(2,1)} async-done(((bf16[64,1,1536]{2,0,1:T(8,128)(2,1)}), bf16[1024,1,1536]{2,0,1:T(8,128)(2,1)}) %all-gather.3.cloned.1.call-update) | async-done | bytes 3145744 | tf_op jit(solution)/shard_map/all_gather | solution.py:201
  90.5 8.6 %shard_map.120 = (bf16[16,1152,128]{2,1,0:T(8,128)(2,1)}, bf16[2,512,768]{2,1,0:T(8,128)(2,1)S(1)}, f32[512,1]{1,0:T(8,128)S(1)}) custom-call(f32[8,2]{1,0:T(8,128)S(1)} %copy.50.gu_scale, f32[6]{0:T(128)S(1)} %select_reduce_fusion.3.d_scale, bf16[512,1024]{1,0:T(8,128)(2,1)S(1)} %bitcast.43, bf16[1024,512]{1,0:T(8,128)(2,1)S(1)} %bitcast.45, ...), custom_call_target="tpu_custom_call" | custom-call | flops 4026531840 | bytes 14680064 | tf_op jit(solution)/shard_map/pallas_call | solution.py:107
  99.1 1.1 copy-done.3
  101.0 1.2 reduce
  102.9 7.6 %all-to-all-start.2 = ((f32[32,1,16]{2,1,0:T(1,128)}), f32[32,1,16]{2,1,0:T(1,128)}, u32[]{:S(2)}, u32[]{:S(2)}) async-start(f32[32,1,16]{2,1,0:T(1,128)} %bitcast.58), calls=%async_computation.3 | async-start | bytes 32768 | tf_op jit(solution)/shard_map/all_to_all | solution.py:229
  110.5 1.4 copy-done.4
  111.9 3.7 %shard_map.121 = bf16[512,1024]{1,0:T(8,128)(2,1)S(1)} custom-call(f32[8,2]{1,0:T(8,128)S(1)} %copy.50.gu_scale, bf16[2,512,768]{2,1,0:T(8,128)(2,1)S(1)} %copy-done.4, bf16[1024,1536]{1,0:T(8,128)(2,1)S(1)} %bitcast.40, bf16[1024,1536]{1,0:T(8,128)(2,1)S(1)} %bitcast.41), custom_call_target="tpu_custom_call" | custom-call | flops 1610612736 | bytes 6291456 | tf_op jit(solution)/shard_map/pallas_call | solution.py:163
  115.7 1.0 copy-done.2
  116.6 7.5 %all-to-all-start.1 = ((bf16[32,16,1024]{2,1,0:T(8,128)(2,1)}), bf16[32,16,1024]{2,1,0:T(8,128)(2,1)S(1)}, u32[]{:S(2)}, u32[]{:S(2)}) async-start(bf16[32,16,1024]{2,1,0:T(8,128)(2,1)} %bitcast.44), calls=%async_computation.2 | async-start | bytes 2097152 | tf_op jit(solution)/shard_map/all_to_all | solution.py:228
  124.7 1.4 reduce.4
  127.0 11.8 %all-to-all-done.1 = bf16[32,16,1024]{2,1,0:T(8,128)(2,1)S(1)} async-done(((bf16[32,16,1024]{2,1,0:T(8,128)(2,1)}), bf16[32,16,1024]{2,1,0:T(8,128)(2,1)S(1)}, u32[]{:S(2)}, u32[]{:S(2)}) %all-to-all-start.1) | async-done | bytes 1048608 | tf_op jit(solution)/shard_map/all_to_all | solution.py:228
  138.8 1.0 convolution_convert_fusion.2
  139.8 40.2 %reduce-scatter.2.cloned.1.call-done = bf16[1,1152,128]{2,1,0:T(8,128)(2,1)} async-done(((bf16[16,1152,128]{2,1,0:T(8,128)(2,1)}), bf16[1,1152,128]{2,1,0:T(8,128)(2,1)}) %reduce-scatter.2.cloned.1.call-update) | async-done | bytes 294928 | tf_op jit(solution)/shard_map/reduce_scatter | solution.py:226
  180.0 0.9 slice.37
  180.9 0.9 slice.36
  181.9 32.5 %all_gather.13 = bf16[3,128,1024]{2,1,0:T(8,128)(2,1)S(1)} all-gather(bf16[3,16,1024]{2,1,0:T(8,128)(2,1)S(1)} %bitcast.55), channel_id=1, replica_groups={{0,64,128,192,256,320,384,448},{32,96,160,224,288,352,416,480},{1,65,12..., dimensions={1}, use_global_device_ids=true | all-gather | bytes 884736 | tf_op jit(solution)/shard_map/all_gather | solution.py:257
  214.5 8.5 %all_gather.14 = bf16[3,256,512]{2,1,0:T(8,128)(2,1)S(1)} all-gather(bf16[3,128,512]{2,1,0:T(8,128)(2,1)S(1)} %get-tuple-element.18), channel_id=1, replica_groups={{0,32},{64,96},{128,160},{192,224},{256,288},{320,352},{384,416},{448,4..., dimensions={1}, use_global_device_ids=true | all-gather | bytes 1179648 | tf_op jit(solution)/shard_map/all_gather | solution.py:257
  222.9 8.4 %all_gather.15 = bf16[3,256,512]{2,1,0:T(8,128)(2,1)S(1)} all-gather(bf16[3,128,512]{2,1,0:T(8,128)(2,1)S(1)} %get-tuple-element.19), channel_id=1, replica_groups={{0,32},{64,96},{128,160},{192,224},{256,288},{320,352},{384,416},{448,4..., dimensions={1}, use_global_device_ids=true | all-gather | bytes 1179648 | tf_op jit(solution)/shard_map/all_gather | solution.py:257
  232.3 1.4 pad_maximum_fusion.1
  (50 shorter events, 9.5 us)
Async XLA Ops:
  7.2 3.8 %copy-start = (bf16[128,1024]{1,0:T(8,128)(2,1)S(1)}, bf16[128,1024]{1,0:T(8,128)(2,1)}, u32[]{:S(2)}) copy-start(bf16[128,1024]{1,0:T(8,128)(2,1)} %param.9) | copy-start | bytes 786436
  7.2 4.2 %copy-start.6 = (bf16[128,1024]{1,0:T(8,128)(2,1)S(1)}, bf16[128,1024]{1,0:T(8,128)(2,1)}, u32[]{:S(2)}) copy-start(bf16[128,1024]{1,0:T(8,128)(2,1)} %param.10) | copy-start | bytes 786436
  7.2 83.3 %all-gather.3.cloned.1.call-start = ((), (), s32[]{:S(2)}) async-start(), calls=%async_computation.5 | async-start | bytes 3342336 | tf_op jit(solution)/shard_map/all_gather | solution.py:201
  13.4 10.4 %copy-start.7 = (s32[8,1,2]{0,2,1:T(2,128)S(1)}, s32[8,1,2]{0,2,1:T(2,128)}, u32[]{:S(2)}) copy-start(s32[8,1,2]{0,2,1:T(2,128)} %param.15) | copy-start | bytes 196
  13.4 10.4 %copy-start.8 = (f32[16]{0:T(128)S(1)}, f32[16]{0:T(128)}, u32[]{:S(2)}) copy-start(f32[16]{0:T(128)} %param.17) | copy-start | bytes 196
  13.4 10.7 %copy-start.10 = (s32[1,6]{1,0:T(1,128)S(1)}, s32[1,6]{1,0:T(1,128)}, u32[]{:S(2)}) copy-start(s32[1,6]{1,0:T(1,128)} %param.16) | copy-start | bytes 76
  13.4 36.0 %all-to-all-start = ((bf16[32,32,1024]{2,1,0:T(8,128)(2,1)}), bf16[32,32,1024]{2,1,0:T(8,128)(2,1)}, u32[]{:S(2)}, u32[]{:S(2)}) async-start(bf16[32,32,1024]{2,1,0:T(8,128)(2,1)} %pad_maximum_fusion), calls=%async_computation | async-start | bytes 4194304 | tf_op jit(solution)/shard_map/all_to_all | solution.py:214
  23.8 156.2 %reduce-scatter.2.cloned.1.call-start = ((), (), s32[]{:S(2)}) async-start(), calls=%async_computation.4 | async-start | bytes 5013504 | tf_op jit(solution)/shard_map/reduce_scatter | solution.py:226
  99.1 1.1 copy-start.3
  100.2 0.7 copy-start.5
  100.9 9.6 %copy-start.1 = (bf16[1024,1,1536]{2,0,1:T(8,128)(2,1)S(1)}, bf16[1024,1,1536]{2,0,1:T(8,128)(2,1)}, u32[]{:S(2)}) copy-start(bf16[1024,1,1536]{2,0,1:T(8,128)(2,1)} %all-gather.3.cloned.1.call-done) | copy-start | bytes 9437188
  102.9 13.7 %all-to-all-start.2 = ((f32[32,1,16]{2,1,0:T(1,128)}), f32[32,1,16]{2,1,0:T(1,128)}, u32[]{:S(2)}, u32[]{:S(2)}) async-start(f32[32,1,16]{2,1,0:T(1,128)} %bitcast.58), calls=%async_computation.3 | async-start | bytes 32768 | tf_op jit(solution)/shard_map/all_to_all | solution.py:229
  110.5 1.4 copy-start.4
  115.7 1.0 copy-start.2
  116.6 9.7 %copy-start.9 = (bf16[128,2]{0,1:T(2,128)(2,1)S(1)}, bf16[128,2]{0,1:T(2,128)(2,1)}, u32[]{:S(2)}) copy-start(bf16[128,2]{0,1:T(2,128)(2,1)} %param.12) | copy-start | bytes 1540
  116.6 22.1 %all-to-all-start.1 = ((bf16[32,16,1024]{2,1,0:T(8,128)(2,1)}), bf16[32,16,1024]{2,1,0:T(8,128)(2,1)S(1)}, u32[]{:S(2)}, u32[]{:S(2)}) async-start(bf16[32,16,1024]{2,1,0:T(8,128)(2,1)} %bitcast.44), calls=%async_computation.2 | async-start | bytes 2097152 | tf_op jit(solution)/shard_map/all_to_all | solution.py:228
Sparse Core Ops, SparseCore 0:
  10.1 80.3 all-gather.2
  101.1 78.8 reduce-scatter.1

commit v4 on v3

--- a/solution.py
+++ b/solution.py
@@ -8,6 +8,7 @@
 QBLOCK = 128
 LANES = 128
 FTILE = 256
+EARLY = 3
 bf16 = jnp.bfloat16
 f32 = jnp.float32
 
@@ -45,7 +46,7 @@
 
 
 def hidden_kernel(
-    gu_scale, d_scale, x_ref, xt_ref, g_ref, hg_ref, wg_ref, wu_ref, sums_ref, joint_ref, dots_ref
+    gu_scale, d_scale, x_ref, xt_ref, g_ref, hg_ref, wg_ref, wu_ref, sums_ref, early_ref, joint_ref, dots_ref
 ):
     step = pl.program_id(0)
     x = x_ref[...]
@@ -90,8 +91,9 @@
         piece = part[drows * own : drows * (own + 1), :] * d_scale[
             step * (FTILE // QBLOCK) + drows * own // QBLOCK
         ]
-        for c in range(part.shape[1] // LANES):
-            at = base + c * drows
+        early_ref[drows * own : drows * (own + 1), :] = piece[:, : LANES * EARLY].astype(bf16)
+        for c in range(EARLY, part.shape[1] // LANES):
+            at = base + (c - EARLY) * drows
             sums_ref[r, at : at + drows, :] = piece[:, LANES * c : LANES * (c + 1)].astype(bf16)
 
 
@@ -100,7 +102,7 @@
     hidden = hg.shape[1]
     steps = hidden // FTILE
     rows = width // owners
-    per_step = 2 * (FTILE // LANES) * rows + (FTILE // owners) * (width // LANES)
+    per_step = 2 * (FTILE // LANES) * rows + (FTILE // owners) * (width // LANES - EARLY)
     smem = pl.BlockSpec(memory_space=pltpu.SMEM)
     whole = lambda a: pl.BlockSpec(a.shape, lambda i: (0, 0))
     flops = 2 * slots * width * hidden * 5
@@ -119,22 +121,24 @@
         ],
         out_specs=[
             pl.BlockSpec((owners, per_step, LANES), lambda i: (0, i, 0)),
+            pl.BlockSpec((FTILE, LANES * EARLY), lambda i: (i, 0)),
             pl.BlockSpec((2, slots, FTILE), lambda i: (0, 0, i)),
             pl.BlockSpec((slots, 1), lambda i: (0, 0)),
         ],
         out_shape=[
             jax.ShapeDtypeStruct((owners, per_step * steps, LANES), bf16),
+            jax.ShapeDtypeStruct((hidden, LANES * EARLY), bf16),
             jax.ShapeDtypeStruct((2, slots, hidden), bf16),
             jax.ShapeDtypeStruct((slots, 1), f32),
         ],
-        compiler_params=pltpu.CompilerParams(vmem_limit_bytes=48 * 1024 * 1024),
+        compiler_params=pltpu.CompilerParams(vmem_limit_bytes=60 * 1024 * 1024),
         cost_estimate=pl.CostEstimate(
             flops=flops, bytes_accessed=14 * 1024 * 1024, transcendentals=slots * hidden
         ),
     )(gu_scale, d_scale, x, xt, g, hg, weights, weights)
 
 
-def rows_kernel(gu_scale, joint_ref, wg_ref, wu_ref, out_ref, total):
+def rows_kernel(gu_scale, joint_ref, dots_ref, wg_ref, wu_ref, out_ref, total):
     step = pl.program_id(0)
     contract = (((1,), (1,)), ((), ()))
     part = lax.dot_general(
@@ -153,10 +157,17 @@
 
     @pl.when(step == pl.num_programs(0) - 1)
     def _():
-        out_ref[...] = total[...].astype(bf16)
-
-
-def rows_step(gu_scale, joint, weights):
+        width = total.shape[1]
+        out_ref[:, :width] = total[...].astype(bf16)
+        dots = dots_ref[...]
+        high = dots.astype(bf16).astype(f32)
+        lane = lax.broadcasted_iota(jnp.int32, (dots.shape[0], LANES), 1)
+        out_ref[:, width:] = jnp.where(
+            lane == 0, high, jnp.where(lane == 1, dots - high, 0.0)
+        ).astype(bf16)
+
+
+def rows_step(gu_scale, joint, dots, weights):
     slots, hidden = joint.shape[1:]
     width = weights.shape[0]
     steps = hidden // FTILE
@@ -166,17 +177,18 @@
         in_specs=[
             pl.BlockSpec(memory_space=pltpu.SMEM),
             pl.BlockSpec((2, slots, FTILE), lambda i: (0, 0, i)),
+            pl.BlockSpec((slots, 1), lambda i: (0, 0)),
             pl.BlockSpec((width, FTILE), lambda i: (0, i)),
             pl.BlockSpec((width, FTILE), lambda i, n=steps: (0, n + i)),
         ],
-        out_specs=pl.BlockSpec((slots, width), lambda i: (0, 0)),
-        out_shape=jax.ShapeDtypeStruct((slots, width), bf16),
+        out_specs=pl.BlockSpec((slots, width + LANES), lambda i: (0, 0)),
+        out_shape=jax.ShapeDtypeStruct((slots, width + LANES), bf16),
         scratch_shapes=[pltpu.VMEM((slots, width), f32)],
         compiler_params=pltpu.CompilerParams(vmem_limit_bytes=32 * 1024 * 1024),
         cost_estimate=pl.CostEstimate(
             flops=4 * slots * width * hidden, bytes_accessed=6 * 1024 * 1024, transcendentals=0
         ),
-    )(gu_scale, joint, weights, weights)
+    )(gu_scale, joint, dots, weights, weights)
 
 
 def body(
@@ -222,19 +234,36 @@
     ).astype(bf16)
     hg = jnp.einsum("sd,fd->sf", g, down_eff, preferred_element_type=f32)
 
-    sums, joint, dots = hidden_step(gu_scale, d_scale, x, xt, g, hg, gathered, owners)
+    sums, early, joint, dots = hidden_step(gu_scale, d_scale, x, xt, g, hg, gathered, owners)
     mine = lax.psum_scatter(sums, "dp", scatter_dimension=0, tiled=True)
-    row_grads = rows_step(gu_scale, joint, gathered).reshape(groups, capacity, width)
-    back_rows = lax.all_to_all(row_grads, "expert", split_axis=0, concat_axis=0, tiled=True)
-    back_dots = lax.all_to_all(
-        dots.reshape(groups, capacity), "expert", split_axis=0, concat_axis=0, tiled=True
-    )
-    token_grad = jnp.dot(
-        either, back_rows.reshape(slots, width), preferred_element_type=f32
-    ).astype(bf16)
-    prob_grad = jnp.sum(slot_hits * back_dots.reshape(slots), axis=-1) / route_probs.astype(f32)
-
-    mine, token_grad, prob_grad = lax.optimization_barrier((mine, token_grad, prob_grad))
+    parts = lax.all_to_all(
+        early.reshape(owners, hidden // owners, LANES * EARLY),
+        "dp",
+        split_axis=0,
+        concat_axis=0,
+        tiled=True,
+    )
+    row_grads = rows_step(gu_scale, joint, dots, gathered)
+    row_grads, parts = lax.optimization_barrier((row_grads, parts))
+    back = lax.all_to_all(
+        row_grads.reshape(groups, capacity, width + LANES),
+        "expert",
+        split_axis=0,
+        concat_axis=0,
+        tiled=True,
+    ).reshape(slots, width + LANES)
+    down_early = lax.all_gather(
+        jnp.sum(parts.astype(f32), axis=0).astype(bf16), "dp", axis=0, tiled=True
+    )
+    token_grad = jnp.dot(either, back[:, :width], preferred_element_type=f32).astype(bf16)
+    picked = jnp.einsum(
+        "tks,sl->tkl", slot_hits.astype(bf16), back[:, width:], preferred_element_type=f32
+    )
+    prob_grad = jnp.sum(picked, axis=-1) / route_probs.astype(f32)
+
+    mine, down_early, token_grad, prob_grad = lax.optimization_barrier(
+        (mine, down_early, token_grad, prob_grad)
+    )
     rows = width // owners
     tiles = FTILE // LANES
     mine = mine.reshape(steps, -1, LANES)
@@ -246,22 +275,20 @@
         .reshape(rows, 1, 2 * hidden)
     )
     drows = FTILE // owners
+    late = width - LANES * EARLY
     own = (
         mine[:, cut:]
-        .reshape(steps, width // LANES, drows, LANES)
+        .reshape(steps, late // LANES, drows, LANES)
         .transpose(0, 2, 1, 3)
-        .reshape(steps, drows, width)
+        .reshape(steps, drows, late)
     )
     same_parity = [list(range(k, owners, 2)) for k in range(2)]
     neighbours = [[k, k + 1] for k in range(0, owners, 2)]
     gather = lambda a, sets: lax.all_gather(
         a, "dp", axis=1, tiled=True, axis_index_groups=sets
     )
-    half = gather(own, same_parity)
-    down_grad = jnp.concatenate(
-        [gather(half[:, :, : width // 2], neighbours), gather(half[:, :, width // 2 :], neighbours)],
-        axis=2,
-    ).reshape(1, hidden, width)
+    down_late = gather(gather(own, same_parity), neighbours).reshape(hidden, late)
+    down_grad = jnp.concatenate([down_early, down_late], axis=1)[None]
     return (token_grad, prob_grad, gate_up_grad, down_grad)
 
 

time: 242 us -> 242 us (level)
  waiting for transfers between devices: 113 us -> 81.7 us
  blocking collectives: 49.4 us -> 80.2 us
    all_gather x0 -> x1, blocking collectives: none -> 39.4 us  [body(): lax.all_gather(jnp.sum(parts.astype(f32), axis=0).astype(bf16), 'dp', axi...]
    reduce_scatter x1, waiting for transfers between devices: 40.2 us -> 4.99 us  [body(): mine = lax.psum_scatter(sums, 'dp', scatter_dimension=0, tiled=True)]
    all_gather x3 -> x2, blocking collectives: 49.4 us -> 40.9 us  [body(): lax.all_gather(a, 'dp', axis=1, tiled=True, axis_index_groups=sets)]
    all_to_all x2, waiting for transfers between devices: 11.8 us -> 16.4 us  [the longest x1 16.3 us: body(): lax.all_to_all(early.reshape(owners, hidden // owners, LANES * EARLY), 'd...]
    unnamed x23 -> x29, local copies, waits for them, and re-layouts: 5.03 us -> 4.86 us
where the time goes in v4:
time: 242 us; the launch traced here: 240 us
  waiting for transfers between devices  81.7 us (34%)
  blocking collectives  80.2 us (33%)
  starting transfers between devices  25.5 us (11%)
  between operations  14.3 us (6%)
  Pallas kernels  13.9 us (6%)
  local copies, waits for them, and re-layouts  11.2 us (5%)
  other arithmetic  6.66 us (3%)
  matrix products  6.14 us (3%)
    all_gather x2, blocking collectives, body(): lax.all_gather(a, 'dp', axis=1, tiled=True, axis_index_groups=sets)  40.9 us
    all_gather x1, blocking collectives, body(): lax.all_gather(jnp.sum(parts.astype(f32), axis=0).astype(bf16), 'dp', axi...  39.4 us
    all_gather x1, waiting for transfers between devices, body(): lax.all_gather(gate_up_weight.reshape(gate_up_weight.shape[0], 2 * hidden...  35.2 us
    all_to_all x1, waiting for transfers between devices, body(): lax.all_to_all(send, 'expert', split_axis=0, concat_axis=0, tiled=True)  24.5 us
    all_to_all x1, waiting for transfers between devices, body(): lax.all_to_all(early.reshape(owners, hidden // owners, LANES * EARLY), 'd...  16.3 us
    pallas_call x1, Pallas kernels, hidden_step(): pl.pallas_call(hidden_kernel, grid=(steps,), in_specs=[smem, smem, whole(...  10 us
    all_to_all x1, starting transfers between devices, body(): lax.all_to_all(send, 'expert', split_axis=0, concat_axis=0, tiled=True)  9.68 us
    all_to_all x1, starting transfers between devices, body(): lax.all_to_all(early.reshape(owners, hidden // owners, LANES * EARLY), 'd...  8.24 us
  transfers between devices with their start and end apart: 5, of which 4 were waited for; matrix products, arithmetic and copies ran while one was open for 7% of the time, Pallas kernels for 2%

profile of v4, /device:TPU:6, one launch (start us, length us, event | category | flops | bytes accessed | tf_op | source)
XLA Modules:
  0.0 239.7 jit_solution(10591869596427027984)
XLA Ops:
  11.9 1.6 pad_maximum_fusion
  13.5 9.7 %all-to-all-start = ((bf16[32,32,1024]{2,1,0:T(8,128)(2,1)}), bf16[32,32,1024]{2,1,0:T(8,128)(2,1)S(1)}, u32[]{:S(2)}, u32[]{:S(2)}) async-start(bf16[32,32,1024]{2,1,0:T(8,128)(2,1)} %pad_maximum_fusion), calls=%async_computation | async-start | bytes 4194304 | tf_op jit(solution)/shard_map/all_to_all | solution.py:226
  24.3 24.5 %all-to-all-done = bf16[32,32,1024]{2,1,0:T(8,128)(2,1)S(1)} async-done(((bf16[32,32,1024]{2,1,0:T(8,128)(2,1)}), bf16[32,32,1024]{2,1,0:T(8,128)(2,1)S(1)}, u32[]{:S(2)}, u32[]{:S(2)}) %all-to-all-start) | async-done | bytes 2097184 | tf_op jit(solution)/shard_map/all_to_all | solution.py:226
  48.8 1.2 fusion.14
  50.0 1.3 copy.48
  52.0 3.7 %fusion.1.hg_ref = f32[512,768]{1,0:T(8,128)} fusion(bf16[512,1024]{1,0:T(8,128)(2,1)S(1)} %bitcast.56, bf16[1,768,1024]{2,1,0:T(8,128)(2,1)} %param.14, f32[768]{0:T(1024)S(1)} %broadcast_bitcast_fusion), kind=kOutput, calls=%fused_computation.3 | convolution fusion | flops 807665664 | bytes 4197376 | tf_op jit(solution)/shard_map/sd,fd->sf/dot_general | solution.py:235
  55.7 35.2 %all-gather.3.cloned.1.call-done = bf16[1024,1,1536]{2,0,1:T(8,128)(2,1)} async-done(((bf16[64,1,1536]{2,0,1:T(8,128)(2,1)}), bf16[1024,1,1536]{2,0,1:T(8,128)(2,1)}) %all-gather.3.cloned.1.call-update) | async-done | bytes 3145744 | tf_op jit(solution)/shard_map/all_gather | solution.py:213
  90.9 10.0 %shard_map.120 = (bf16[16,1008,128]{2,1,0:T(8,128)(2,1)}, bf16[768,384]{1,0:T(8,128)(2,1)}, bf16[2,512,768]{2,1,0:T(8,128)(2,1)}, f32[512,1]{1,0:T(8,128)}) custom-call(f32[8,2]{1,0:T(8,128)} %copy.49.gu_scale, f32[6]{0:T(128)} %copy-done.12, bf16[512,1024]{1,0:T(8,128)(2,1)} %bitcast.48, bf16[1024,512]{1,0:T(8,128)(2,1)} %bitcast.54, ...), custom_call_target="tpu_custom_call" | custom-call | flops 4026531840 | bytes 14680064 | tf_op jit(solution)/shard_map/pallas_call | solution.py:109
  100.9 8.2 %all-to-all-start.1 = ((bf16[16,48,384]{2,1,0:T(8,128)(2,1)}), bf16[16,48,384]{2,1,0:T(8,128)(2,1)}, u32[]{:S(2)}, u32[]{:S(2)}) async-start(bf16[16,48,384]{2,1,0:T(8,128)(2,1)} %bitcast.58), calls=%async_computation.2 | async-start | bytes 1179648 | tf_op jit(solution)/shard_map/all_to_all | solution.py:239
  109.2 1.4 copy-done.3
  110.6 0.9 copy-done.4
  111.6 3.8 %shard_map.121 = bf16[512,1152]{1,0:T(8,128)(2,1)S(1)} custom-call(f32[8,2]{1,0:T(8,128)S(1)} %copy-done.5, bf16[2,512,768]{2,1,0:T(8,128)(2,1)S(1)} %copy-done.3, f32[512,1]{1,0:T(8,128)S(1)} %copy-done.4, bf16[1024,1536]{1,0:T(8,128)(2,1)S(1)} %bitcast.44, bf16[1024,1536]{1,0:T(8,128)(2,1)S(1)} %bitcast.45), custom_call_target="tpu_custom_call" | custom-call | flops 1610612736 | bytes 6291456 | tf_op jit(solution)/shard_map/pallas_call | solution.py:174
  115.4 1.0 copy-done.2
  116.4 16.3 %all-to-all-done.1 = bf16[16,48,384]{2,1,0:T(8,128)(2,1)} async-done(((bf16[16,48,384]{2,1,0:T(8,128)(2,1)}), bf16[16,48,384]{2,1,0:T(8,128)(2,1)}, u32[]{:S(2)}, u32[]{:S(2)}) %all-to-all-start.1) | async-done | bytes 589856 | tf_op jit(solution)/shard_map/all_to_all | solution.py:239
  132.8 7.6 %all-to-all-start.2 = ((bf16[32,16,1152]{2,1,0:T(8,128)(2,1)}), bf16[32,16,1152]{2,1,0:T(8,128)(2,1)S(1)}, u32[]{:S(2)}, u32[]{:S(2)}) async-start(bf16[32,16,1152]{2,1,0:T(8,128)(2,1)} %bitcast.46), calls=%async_computation.3 | async-start | bytes 2359296 | tf_op jit(solution)/shard_map/all_to_all | solution.py:248
  140.3 1.2 reduce_sum.64
  141.5 39.4 %all_gather.13 = bf16[768,384]{1,0:T(8,128)(2,1)S(1)} all-gather(bf16[48,384]{1,0:T(8,128)(2,1)S(1)} %reduce_sum.64), channel_id=1, replica_groups=mesh['dp'=16,'expert'=32] {'dp'}, dimensions={0}, use_global_device_ids=true | all-gather | bytes 626688 | tf_op jit(solution)/shard_map/all_gather | solution.py:255
  181.8 1.0 convolution_convert_fusion.2
  182.8 5.0 %reduce-scatter.2.cloned.1.call-done = bf16[1,1008,128]{2,1,0:T(8,128)(2,1)} async-done(((bf16[16,1008,128]{2,1,0:T(8,128)(2,1)}), bf16[1,1008,128]{2,1,0:T(8,128)(2,1)}) %reduce-scatter.2.cloned.1.call-update) | async-done | bytes 258064 | tf_op jit(solution)/shard_map/reduce_scatter | solution.py:238
  187.8 0.8 slice.39
  188.7 0.9 slice.38
  190.6 31.4 %all_gather.14 = bf16[3,128,640]{2,1,0:T(8,128)(2,1)S(1)} all-gather(bf16[3,16,640]{2,1,0:T(8,128)(2,1)S(1)} %bitcast.62), channel_id=1, replica_groups={{0,64,128,192,256,320,384,448},{32,96,160,224,288,352,416,480},{1,65,12..., dimensions={1}, use_global_device_ids=true | all-gather | bytes 552960 | tf_op jit(solution)/shard_map/all_gather | solution.py:287
  221.9 9.5 %all_gather.15 = bf16[3,256,640]{2,1,0:T(8,128)(2,1)S(1)} all-gather(bf16[3,128,640]{2,1,0:T(8,128)(2,1)S(1)} %all_gather.14), channel_id=1, replica_groups={{0,32},{64,96},{128,160},{192,224},{256,288},{320,352},{384,416},{448,4..., dimensions={1}, use_global_device_ids=true | all-gather | bytes 1474560 | tf_op jit(solution)/shard_map/all_gather | solution.py:287
  231.4 1.4 maximum_bitcast_fusion
  (51 shorter events, 8.3 us)
Async XLA Ops:
  7.2 3.8 %copy-start = (bf16[128,1024]{1,0:T(8,128)(2,1)S(1)}, bf16[128,1024]{1,0:T(8,128)(2,1)}, u32[]{:S(2)}) copy-start(bf16[128,1024]{1,0:T(8,128)(2,1)} %param.10) | copy-start | bytes 786436
  7.2 4.2 %copy-start.8 = (bf16[128,1024]{1,0:T(8,128)(2,1)S(1)}, bf16[128,1024]{1,0:T(8,128)(2,1)}, u32[]{:S(2)}) copy-start(bf16[128,1024]{1,0:T(8,128)(2,1)} %param.9) | copy-start | bytes 786436
  7.2 83.7 %all-gather.3.cloned.1.call-start = ((), (), s32[]{:S(2)}) async-start(), calls=%async_computation.5 | async-start | bytes 3342336 | tf_op jit(solution)/shard_map/all_gather | solution.py:213
  13.5 9.7 %copy-start.9 = (s32[8,1,2]{0,2,1:T(2,128)S(1)}, s32[8,1,2]{0,2,1:T(2,128)}, u32[]{:S(2)}) copy-start(s32[8,1,2]{0,2,1:T(2,128)} %param.15) | copy-start | bytes 196
  13.5 9.8 %copy-start.10 = (f32[16]{0:T(128)S(1)}, f32[16]{0:T(128)}, u32[]{:S(2)}) copy-start(f32[16]{0:T(128)} %param.17) | copy-start | bytes 196
  13.5 10.6 %copy-start.13 = (s32[1,6]{1,0:T(1,128)S(1)}, s32[1,6]{1,0:T(1,128)}, u32[]{:S(2)}) copy-start(s32[1,6]{1,0:T(1,128)} %param.16) | copy-start | bytes 76
  13.5 35.3 %all-to-all-start = ((bf16[32,32,1024]{2,1,0:T(8,128)(2,1)}), bf16[32,32,1024]{2,1,0:T(8,128)(2,1)S(1)}, u32[]{:S(2)}, u32[]{:S(2)}) async-start(bf16[32,32,1024]{2,1,0:T(8,128)(2,1)} %pad_maximum_fusion), calls=%async_computation | async-start | bytes 4194304 | tf_op jit(solution)/shard_map/all_to_all | solution.py:226
  23.1 164.7 %reduce-scatter.2.cloned.1.call-start = ((), (), s32[]{:S(2)}) async-start(), calls=%async_computation.4 | async-start | bytes 4386816 | tf_op jit(solution)/shard_map/reduce_scatter | solution.py:238
  24.2 25.8 %copy-start.12 = (f32[6]{0:T(128)}, f32[6]{0:T(128)S(1)}, u32[]{:S(2)}) copy-start(f32[6]{0:T(128)S(1)} %select_reduce_fusion.2.d_scale) | copy-start | bytes 76
  50.0 5.7 %copy-start.6 = (bf16[32,16,1024]{2,1,0:T(8,128)(2,1)}, bf16[32,16,1024]{2,1,0:T(8,128)(2,1)S(1)}, u32[]{:S(2)}) copy-start(bf16[32,16,1024]{2,1,0:T(8,128)(2,1)S(1)} %get-tuple-element.25) | copy-start | bytes 3145732
  50.0 2.0 copy-start.7
  100.9 8.3 %copy-start.1 = (bf16[1024,1,1536]{2,0,1:T(8,128)(2,1)S(1)}, bf16[1024,1,1536]{2,0,1:T(8,128)(2,1)}, u32[]{:S(2)}) copy-start(bf16[1024,1,1536]{2,0,1:T(8,128)(2,1)} %all-gather.3.cloned.1.call-done) | copy-start | bytes 9437188
  100.9 8.3 %copy-start.5 = (f32[8,2]{1,0:T(8,128)S(1)}, f32[8,2]{1,0:T(8,128)}, u32[]{:S(2)}) copy-start(f32[8,2]{1,0:T(8,128)} %copy.49.gu_scale) | copy-start | bytes 196
  100.9 31.8 %all-to-all-start.1 = ((bf16[16,48,384]{2,1,0:T(8,128)(2,1)}), bf16[16,48,384]{2,1,0:T(8,128)(2,1)}, u32[]{:S(2)}, u32[]{:S(2)}) async-start(bf16[16,48,384]{2,1,0:T(8,128)(2,1)} %bitcast.58), calls=%async_computation.2 | async-start | bytes 1179648 | tf_op jit(solution)/shard_map/all_to_all | solution.py:239
  109.2 1.4 copy-start.3
  110.6 0.9 copy-start.4
  115.4 1.0 copy-start.2
  116.4 64.8 %copy-start.11 = (bf16[128,2]{0,1:T(2,128)(2,1)S(1)}, bf16[128,2]{0,1:T(2,128)(2,1)}, u32[]{:S(2)}) copy-start(bf16[128,2]{0,1:T(2,128)(2,1)} %param.12) | copy-start | bytes 1540
  132.8 48.1 %all-to-all-start.2 = ((bf16[32,16,1152]{2,1,0:T(8,128)(2,1)}), bf16[32,16,1152]{2,1,0:T(8,128)(2,1)S(1)}, u32[]{:S(2)}, u32[]{:S(2)}) async-start(bf16[32,16,1152]{2,1,0:T(8,128)(2,1)} %bitcast.46), calls=%async_computation.3 | async-start | bytes 2359296 | tf_op jit(solution)/shard_map/all_to_all | solution.py:248
Sparse Core Ops, SparseCore 0:
  10.1 80.7 all-gather.2
  101.1 86.7 reduce-scatter.1

commit v5 on v4

--- a/solution.py
+++ b/solution.py
@@ -55,7 +55,7 @@
     sig = jax.nn.sigmoid(gate)
     act = gate * sig
     hidden = (act * up).astype(bf16)
-    hg = hg_ref[...]
+    hg = hg_ref[:, pl.ds(pl.multiple_of(step * FTILE, FTILE), FTILE)]
     joint = (
         (hg * up * sig * (1.0 + gate * (1.0 - sig))).astype(bf16),
         (hg * act).astype(bf16),
@@ -87,11 +87,10 @@
     drows = FTILE // owners
     base = 2 * (FTILE // LANES) * rows
     for r in range(owners):
-        own = (r % 2) * (owners // 2) + r // 2
-        piece = part[drows * own : drows * (own + 1), :] * d_scale[
-            step * (FTILE // QBLOCK) + drows * own // QBLOCK
+        piece = part[drows * r : drows * (r + 1), :] * d_scale[
+            step * (FTILE // QBLOCK) + drows * r // QBLOCK
         ]
-        early_ref[drows * own : drows * (own + 1), :] = piece[:, : LANES * EARLY].astype(bf16)
+        early_ref[drows * r : drows * (r + 1), :] = piece[:, : LANES * EARLY].astype(bf16)
         for c in range(EARLY, part.shape[1] // LANES):
             at = base + (c - EARLY) * drows
             sums_ref[r, at : at + drows, :] = piece[:, LANES * c : LANES * (c + 1)].astype(bf16)
@@ -104,7 +103,7 @@
     rows = width // owners
     per_step = 2 * (FTILE // LANES) * rows + (FTILE // owners) * (width // LANES - EARLY)
     smem = pl.BlockSpec(memory_space=pltpu.SMEM)
-    whole = lambda a: pl.BlockSpec(a.shape, lambda i: (0, 0))
+    vmem = pl.BlockSpec(memory_space=pltpu.VMEM)
     flops = 2 * slots * width * hidden * 5
     return pl.pallas_call(
         hidden_kernel,
@@ -112,10 +111,10 @@
         in_specs=[
             smem,
             smem,
-            whole(x),
-            whole(xt),
-            whole(g),
-            pl.BlockSpec((slots, FTILE), lambda i: (0, i)),
+            vmem,
+            vmem,
+            vmem,
+            vmem,
             pl.BlockSpec((width, FTILE), lambda i: (0, i)),
             pl.BlockSpec((width, FTILE), lambda i, n=steps: (0, n + i)),
         ],
@@ -126,12 +125,12 @@
             pl.BlockSpec((slots, 1), lambda i: (0, 0)),
         ],
         out_shape=[
-            jax.ShapeDtypeStruct((owners, per_step * steps, LANES), bf16),
-            jax.ShapeDtypeStruct((hidden, LANES * EARLY), bf16),
-            jax.ShapeDtypeStruct((2, slots, hidden), bf16),
-            jax.ShapeDtypeStruct((slots, 1), f32),
+            pltpu.HBM((owners, per_step * steps, LANES), bf16),
+            pltpu.HBM((hidden, LANES * EARLY), bf16),
+            pltpu.HBM((2, slots, hidden), bf16),
+            pltpu.HBM((slots, 1), f32),
         ],
-        compiler_params=pltpu.CompilerParams(vmem_limit_bytes=60 * 1024 * 1024),
+        compiler_params=pltpu.CompilerParams(vmem_limit_bytes=48 * 1024 * 1024),
         cost_estimate=pl.CostEstimate(
             flops=flops, bytes_accessed=14 * 1024 * 1024, transcendentals=slots * hidden
         ),
@@ -276,18 +275,14 @@
     )
     drows = FTILE // owners
     late = width - LANES * EARLY
+    late = width - LANES * EARLY
     own = (
         mine[:, cut:]
         .reshape(steps, late // LANES, drows, LANES)
         .transpose(0, 2, 1, 3)
         .reshape(steps, drows, late)
     )
-    same_parity = [list(range(k, owners, 2)) for k in range(2)]
-    neighbours = [[k, k + 1] for k in range(0, owners, 2)]
-    gather = lambda a, sets: lax.all_gather(
-        a, "dp", axis=1, tiled=True, axis_index_groups=sets
-    )
-    down_late = gather(gather(own, same_parity), neighbours).reshape(hidden, late)
+    down_late = lax.all_gather(own, "dp", axis=1, tiled=True).reshape(hidden, late)
     down_grad = jnp.concatenate([down_early, down_late], axis=1)[None]
     return (token_grad, prob_grad, gate_up_grad, down_grad)
 

time: 242 us -> 234 us (0.967)
  blocking collectives: 80.2 us -> 72.5 us
    all_gather x2 -> x1, blocking collectives: 40.9 us -> 33.5 us  [body(): lax.all_gather(own, 'dp', axis=1, tiled=True).reshape(hidden, late)]
    unnamed x29 -> x23, local copies, waits for them, and re-layouts: 4.86 us -> 5.58 us
  transfers between devices with their start and end apart: 5 -> 5, of which waited for: 4 -> 4; matrix products, arithmetic and copies ran while one was open for 7% -> 6% of each run, Pallas kernels for 2% -> 2%
where the time goes in v5:
time: 234 us; the launch traced here: 233 us
  waiting for transfers between devices  83.9 us (36%)
  blocking collectives  72.5 us (31%)
  starting transfers between devices  26.2 us (11%)
  between operations  14.3 us (6%)
  Pallas kernels  12.5 us (5%)
  local copies, waits for them, and re-layouts  11.1 us (5%)
  other arithmetic  6.68 us (3%)
  matrix products  6.16 us (3%)
    all_gather x1, blocking collectives, body(): lax.all_gather(jnp.sum(parts.astype(f32), axis=0).astype(bf16), 'dp', axi...  39.1 us
    all_gather x1, waiting for transfers between devices, body(): lax.all_gather(gate_up_weight.reshape(gate_up_weight.shape[0], 2 * hidden...  35 us
    all_gather x1, blocking collectives, body(): lax.all_gather(own, 'dp', axis=1, tiled=True).reshape(hidden, late)  33.5 us
    all_to_all x1, waiting for transfers between devices, body(): lax.all_to_all(send, 'expert', split_axis=0, concat_axis=0, tiled=True)  25.1 us
    all_to_all x1, waiting for transfers between devices, body(): lax.all_to_all(early.reshape(owners, hidden // owners, LANES * EARLY), 'd...  18 us
    all_to_all x1, starting transfers between devices, body(): lax.all_to_all(send, 'expert', split_axis=0, concat_axis=0, tiled=True)  10.4 us
    pallas_call x1, Pallas kernels, hidden_step(): pl.pallas_call(hidden_kernel, grid=(steps,), in_specs=[smem, smem, vmem,...  8.65 us
    all_to_all x1, starting transfers between devices, body(): lax.all_to_all(early.reshape(owners, hidden // owners, LANES * EARLY), 'd...  8.43 us
  transfers between devices with their start and end apart: 5, of which 4 were waited for; matrix products, arithmetic and copies ran while one was open for 6% of the time, Pallas kernels for 2%

profile of v5, /device:TPU:6, one launch (start us, length us, event | category | flops | bytes accessed | tf_op | source)
XLA Modules:
  0.0 233.3 jit_solution(13476795371735672634)
XLA Ops:
  8.6 0.8 copy.46
  11.9 1.6 pad_maximum_fusion
  13.5 10.4 %all-to-all-start = ((bf16[32,32,1024]{2,1,0:T(8,128)(2,1)}), bf16[32,32,1024]{2,1,0:T(8,128)(2,1)}, u32[]{:S(2)}, u32[]{:S(2)}) async-start(bf16[32,32,1024]{2,1,0:T(8,128)(2,1)} %pad_maximum_fusion), calls=%async_computation | async-start | bytes 4194304 | tf_op jit(solution)/shard_map/all_to_all | solution.py:225
  24.4 25.1 %all-to-all-done = bf16[32,32,1024]{2,1,0:T(8,128)(2,1)} async-done(((bf16[32,32,1024]{2,1,0:T(8,128)(2,1)}), bf16[32,32,1024]{2,1,0:T(8,128)(2,1)}, u32[]{:S(2)}, u32[]{:S(2)}) %all-to-all-start) | async-done | bytes 2097184 | tf_op jit(solution)/shard_map/all_to_all | solution.py:225
  49.5 1.7 fusion.14
  51.8 3.7 %fusion.1.hg_ref = f32[512,768]{1,0:T(8,128)} fusion(bf16[512,1024]{1,0:T(8,128)(2,1)S(1)} %bitcast.50, bf16[1,768,1024]{2,1,0:T(8,128)(2,1)} %param.14, f32[768]{0:T(1024)S(1)} %broadcast_bitcast_fusion), kind=kOutput, calls=%fused_computation.3 | convolution fusion | flops 807665664 | bytes 4197376 | tf_op jit(solution)/shard_map/sd,fd->sf/dot_general | solution.py:234
  55.5 35.0 %all-gather.3.cloned.1.call-done = bf16[1024,1,1536]{2,0,1:T(8,128)(2,1)} async-done(((bf16[64,1,1536]{2,0,1:T(8,128)(2,1)}), bf16[1024,1,1536]{2,0,1:T(8,128)(2,1)}) %all-gather.3.cloned.1.call-update) | async-done | bytes 3145744 | tf_op jit(solution)/shard_map/all_gather | solution.py:212
  90.5 1.4 copy-done.5
  91.9 8.6 %shard_map.120 = (bf16[16,1008,128]{2,1,0:T(8,128)(2,1)}, bf16[768,384]{1,0:T(8,128)(2,1)}, bf16[2,512,768]{2,1,0:T(8,128)(2,1)}, f32[512,1]{1,0:T(8,128)}) custom-call(f32[8,2]{1,0:T(8,128)S(1)} %copy.49.gu_scale, f32[6]{0:T(128)S(1)} %select_reduce_fusion.2.d_scale, bf16[512,1024]{1,0:T(8,128)(2,1)S(1)} %bitcast.48, bf16[1024,512]{1,0:T(8,128)(2,1)S(1)} %bitcast.49, ...), custom_call_target="tpu_custom_call" | custom-call | flops 4026531840 | bytes 14680064 | tf_op jit(solution)/shard_map/pallas_call | solution.py:108
  100.6 8.4 %all-to-all-start.1 = ((bf16[16,48,384]{2,1,0:T(8,128)(2,1)}), bf16[16,48,384]{2,1,0:T(8,128)(2,1)}, u32[]{:S(2)}, u32[]{:S(2)}) async-start(bf16[16,48,384]{2,1,0:T(8,128)(2,1)} %bitcast.58), calls=%async_computation.2 | async-start | bytes 1179648 | tf_op jit(solution)/shard_map/all_to_all | solution.py:238
  109.0 1.4 copy-done.3
  110.4 0.9 copy-done.4
  111.4 3.8 %shard_map.121 = bf16[512,1152]{1,0:T(8,128)(2,1)S(1)} custom-call(f32[8,2]{1,0:T(8,128)S(1)} %copy.49.gu_scale, bf16[2,512,768]{2,1,0:T(8,128)(2,1)S(1)} %copy-done.3, f32[512,1]{1,0:T(8,128)S(1)} %copy-done.4, bf16[1024,1536]{1,0:T(8,128)(2,1)S(1)} %bitcast.44, bf16[1024,1536]{1,0:T(8,128)(2,1)S(1)} %bitcast.45), custom_call_target="tpu_custom_call" | custom-call | flops 1610612736 | bytes 6291456 | tf_op jit(solution)/shard_map/pallas_call | solution.py:173
  115.2 1.0 copy-done.2
  116.2 18.0 %all-to-all-done.1 = bf16[16,48,384]{2,1,0:T(8,128)(2,1)} async-done(((bf16[16,48,384]{2,1,0:T(8,128)(2,1)}), bf16[16,48,384]{2,1,0:T(8,128)(2,1)}, u32[]{:S(2)}, u32[]{:S(2)}) %all-to-all-start.1) | async-done | bytes 589856 | tf_op jit(solution)/shard_map/all_to_all | solution.py:238
  134.3 7.3 %all-to-all-start.2 = ((bf16[32,16,1152]{2,1,0:T(8,128)(2,1)}), bf16[32,16,1152]{2,1,0:T(8,128)(2,1)S(1)}, u32[]{:S(2)}, u32[]{:S(2)}) async-start(bf16[32,16,1152]{2,1,0:T(8,128)(2,1)} %bitcast.46), calls=%async_computation.3 | async-start | bytes 2359296 | tf_op jit(solution)/shard_map/all_to_all | solution.py:247
  141.6 1.2 reduce_sum.64
  142.7 39.1 %all_gather.10 = bf16[768,384]{1,0:T(8,128)(2,1)S(1)} all-gather(bf16[48,384]{1,0:T(8,128)(2,1)S(1)} %reduce_sum.64), channel_id=1, replica_groups=mesh['dp'=16,'expert'=32] {'dp'}, dimensions={0}, use_global_device_ids=true | all-gather | bytes 626688 | tf_op jit(solution)/shard_map/all_gather | solution.py:254
  182.8 1.0 convolution_convert_fusion.2
  183.8 5.1 %reduce-scatter.2.cloned.1.call-done = bf16[1,1008,128]{2,1,0:T(8,128)(2,1)} async-done(((bf16[16,1008,128]{2,1,0:T(8,128)(2,1)}), bf16[1,1008,128]{2,1,0:T(8,128)(2,1)}) %reduce-scatter.2.cloned.1.call-update) | async-done | bytes 258064 | tf_op jit(solution)/shard_map/reduce_scatter | solution.py:237
  188.9 0.8 slice.39
  189.7 0.9 slice.38
  191.6 33.5 %all_gather.11 = bf16[3,256,640]{2,1,0:T(8,128)(2,1)S(1)} all-gather(bf16[3,16,640]{2,1,0:T(8,128)(2,1)S(1)} %bitcast.62), channel_id=1, replica_groups=mesh['dp'=16,'expert'=32] {'dp'}, dimensions={1}, use_global_device_ids=true | all-gather | bytes 1044480 | tf_op jit(solution)/shard_map/all_gather | solution.py:285
  225.1 1.4 maximum_bitcast_fusion
  (44 shorter events, 6.8 us)
Async XLA Ops:
  7.2 3.8 %copy-start = (bf16[128,1024]{1,0:T(8,128)(2,1)S(1)}, bf16[128,1024]{1,0:T(8,128)(2,1)}, u32[]{:S(2)}) copy-start(bf16[128,1024]{1,0:T(8,128)(2,1)} %param.10) | copy-start | bytes 786436
  7.2 4.2 %copy-start.6 = (bf16[128,1024]{1,0:T(8,128)(2,1)S(1)}, bf16[128,1024]{1,0:T(8,128)(2,1)}, u32[]{:S(2)}) copy-start(bf16[128,1024]{1,0:T(8,128)(2,1)} %param.9) | copy-start | bytes 786436
  7.2 83.3 %all-gather.3.cloned.1.call-start = ((), (), s32[]{:S(2)}) async-start(), calls=%async_computation.5 | async-start | bytes 3342336 | tf_op jit(solution)/shard_map/all_gather | solution.py:212
  13.5 10.4 %copy-start.7 = (s32[8,1,2]{0,2,1:T(2,128)S(1)}, s32[8,1,2]{0,2,1:T(2,128)}, u32[]{:S(2)}) copy-start(s32[8,1,2]{0,2,1:T(2,128)} %param.15) | copy-start | bytes 196
  13.5 10.4 %copy-start.8 = (f32[16]{0:T(128)S(1)}, f32[16]{0:T(128)}, u32[]{:S(2)}) copy-start(f32[16]{0:T(128)} %param.17) | copy-start | bytes 196
  13.5 10.7 %copy-start.10 = (s32[1,6]{1,0:T(1,128)S(1)}, s32[1,6]{1,0:T(1,128)}, u32[]{:S(2)}) copy-start(s32[1,6]{1,0:T(1,128)} %param.16) | copy-start | bytes 76
  13.5 36.1 %all-to-all-start = ((bf16[32,32,1024]{2,1,0:T(8,128)(2,1)}), bf16[32,32,1024]{2,1,0:T(8,128)(2,1)}, u32[]{:S(2)}, u32[]{:S(2)}) async-start(bf16[32,32,1024]{2,1,0:T(8,128)(2,1)} %pad_maximum_fusion), calls=%async_computation | async-start | bytes 4194304 | tf_op jit(solution)/shard_map/all_to_all | solution.py:225
  23.9 165.0 %reduce-scatter.2.cloned.1.call-start = ((), (), s32[]{:S(2)}) async-start(), calls=%async_computation.4 | async-start | bytes 4386816 | tf_op jit(solution)/shard_map/reduce_scatter | solution.py:237
  90.5 1.4 copy-start.5
  100.5 8.5 %copy-start.1 = (bf16[1024,1,1536]{2,0,1:T(8,128)(2,1)S(1)}, bf16[1024,1,1536]{2,0,1:T(8,128)(2,1)}, u32[]{:S(2)}) copy-start(bf16[1024,1,1536]{2,0,1:T(8,128)(2,1)} %all-gather.3.cloned.1.call-done) | copy-start | bytes 9437188
  100.6 33.7 %all-to-all-start.1 = ((bf16[16,48,384]{2,1,0:T(8,128)(2,1)}), bf16[16,48,384]{2,1,0:T(8,128)(2,1)}, u32[]{:S(2)}, u32[]{:S(2)}) async-start(bf16[16,48,384]{2,1,0:T(8,128)(2,1)} %bitcast.58), calls=%async_computation.2 | async-start | bytes 1179648 | tf_op jit(solution)/shard_map/all_to_all | solution.py:238
  109.0 1.4 copy-start.3
  110.4 0.9 copy-start.4
  115.2 1.0 copy-start.2
  116.2 65.9 %copy-start.9 = (bf16[128,2]{0,1:T(2,128)(2,1)S(1)}, bf16[128,2]{0,1:T(2,128)(2,1)}, u32[]{:S(2)}) copy-start(bf16[128,2]{0,1:T(2,128)(2,1)} %param.12) | copy-start | bytes 1540
  134.3 47.6 %all-to-all-start.2 = ((bf16[32,16,1152]{2,1,0:T(8,128)(2,1)}), bf16[32,16,1152]{2,1,0:T(8,128)(2,1)S(1)}, u32[]{:S(2)}, u32[]{:S(2)}) async-start(bf16[32,16,1152]{2,1,0:T(8,128)(2,1)} %bitcast.46), calls=%async_computation.3 | async-start | bytes 2359296 | tf_op jit(solution)/shard_map/all_to_all | solution.py:247
Sparse Core Ops, SparseCore 0:
  10.1 80.3 all-gather.2
  100.7 88.1 reduce-scatter.1

commit v6 on v5

--- a/solution.py
+++ b/solution.py
@@ -1,3 +1,5 @@
+import functools
+
 import jax
 import jax.numpy as jnp
 from jax import lax
@@ -55,7 +57,7 @@
     sig = jax.nn.sigmoid(gate)
     act = gate * sig
     hidden = (act * up).astype(bf16)
-    hg = hg_ref[:, pl.ds(pl.multiple_of(step * FTILE, FTILE), FTILE)]
+    hg = hg_ref[...]
     joint = (
         (hg * up * sig * (1.0 + gate * (1.0 - sig))).astype(bf16),
         (hg * act).astype(bf16),
@@ -114,7 +116,7 @@
             vmem,
             vmem,
             vmem,
-            vmem,
+            pl.BlockSpec((slots, FTILE), lambda i: (0, i)),
             pl.BlockSpec((width, FTILE), lambda i: (0, i)),
             pl.BlockSpec((width, FTILE), lambda i, n=steps: (0, n + i)),
         ],
@@ -134,7 +136,7 @@
         cost_estimate=pl.CostEstimate(
             flops=flops, bytes_accessed=14 * 1024 * 1024, transcendentals=slots * hidden
         ),
-    )(gu_scale, d_scale, x, xt, g, hg, weights, weights)
+    )(gu_scale, d_scale, x, xt, g, pltpu.with_memory_space_constraint(hg, pltpu.HBM), weights, weights)
 
 
 def rows_kernel(gu_scale, joint_ref, dots_ref, wg_ref, wu_ref, out_ref, total):
@@ -188,6 +190,33 @@
             flops=4 * slots * width * hidden, bytes_accessed=6 * 1024 * 1024, transcendentals=0
         ),
     )(gu_scale, joint, dots, weights, weights)
+
+
+def layout_kernel(hidden, mine_ref, gate_up_ref, own_ref):
+    rows = gate_up_ref.shape[0]
+    steps, drows, late = own_ref.shape
+    tiles = FTILE // LANES
+    for i in range(steps):
+        for k in range(2):
+            for c in range(tiles):
+                at = (tiles * k + c) * rows
+                to = hidden * k + FTILE * i + LANES * c
+                gate_up_ref[:, to : to + LANES] = mine_ref[i, at : at + rows, :]
+        for c in range(late // LANES):
+            at = 2 * tiles * rows + c * drows
+            own_ref[i, :, LANES * c : LANES * (c + 1)] = mine_ref[i, at : at + drows, :]
+
+
+def layout_step(mine, hidden, rows, drows, late):
+    steps = mine.shape[0]
+    return pl.pallas_call(
+        functools.partial(layout_kernel, hidden),
+        out_shape=[
+            jax.ShapeDtypeStruct((rows, 2 * hidden), bf16),
+            jax.ShapeDtypeStruct((steps, drows, late), bf16),
+        ],
+        cost_estimate=pl.CostEstimate(flops=0, bytes_accessed=1024 * 1024, transcendentals=0),
+    )(mine)
 
 
 def body(
@@ -263,25 +292,11 @@
     mine, down_early, token_grad, prob_grad = lax.optimization_barrier(
         (mine, down_early, token_grad, prob_grad)
     )
-    rows = width // owners
-    tiles = FTILE // LANES
-    mine = mine.reshape(steps, -1, LANES)
-    cut = 2 * tiles * rows
-    gate_up_grad = (
-        mine[:, :cut]
-        .reshape(steps, 2, tiles, rows, LANES)
-        .transpose(3, 1, 0, 2, 4)
-        .reshape(rows, 1, 2 * hidden)
-    )
-    drows = FTILE // owners
     late = width - LANES * EARLY
-    late = width - LANES * EARLY
-    own = (
-        mine[:, cut:]
-        .reshape(steps, late // LANES, drows, LANES)
-        .transpose(0, 2, 1, 3)
-        .reshape(steps, drows, late)
-    )
+    gate_up_grad, own = layout_step(
+        mine.reshape(steps, -1, LANES), hidden, width // owners, FTILE // owners, late
+    )
+    gate_up_grad = gate_up_grad[:, None, :]
     down_late = lax.all_gather(own, "dp", axis=1, tiled=True).reshape(hidden, late)
     down_grad = jnp.concatenate([down_early, down_late], axis=1)[None]
     return (token_grad, prob_grad, gate_up_grad, down_grad)

time: 234 us -> 232 us (level)
  local copies, waits for them, and re-layouts: 11.1 us -> 6.93 us
    unnamed x23 -> x21, local copies, waits for them, and re-layouts: 5.58 us -> 4.18 us
  transfers between devices with their start and end apart: 5 -> 5, of which waited for: 4 -> 4; matrix products, arithmetic and copies ran while one was open for 6% -> 7% of each run, Pallas kernels for 2% -> 2%
where the time goes in v6:
time: 232 us; the launch traced here: 231 us
  waiting for transfers between devices  84.8 us (37%)
  blocking collectives  71.5 us (31%)
  starting transfers between devices  26.2 us (11%)
  Pallas kernels  14.4 us (6%)
  between operations  14.2 us (6%)
  local copies, waits for them, and re-layouts  6.93 us (3%)
  other arithmetic  6.69 us (3%)
  matrix products  6.15 us (3%)
    all_gather x1, blocking collectives, body(): lax.all_gather(jnp.sum(parts.astype(f32), axis=0).astype(bf16), 'dp', axi...  38 us
    all_gather x1, waiting for transfers between devices, body(): lax.all_gather(gate_up_weight.reshape(gate_up_weight.shape[0], 2 * hidden...  35 us
    all_gather x1, blocking collectives, body(): lax.all_gather(own, 'dp', axis=1, tiled=True).reshape(hidden, late)  33.5 us
    all_to_all x1, waiting for transfers between devices, body(): lax.all_to_all(send, 'expert', split_axis=0, concat_axis=0, tiled=True)  25.1 us
    all_to_all x1, waiting for transfers between devices, body(): lax.all_to_all(early.reshape(owners, hidden // owners, LANES * EARLY), 'd...  18 us
    all_to_all x1, starting transfers between devices, body(): lax.all_to_all(send, 'expert', split_axis=0, concat_axis=0, tiled=True)  10.4 us
    pallas_call x1, Pallas kernels, hidden_step(): pl.pallas_call(hidden_kernel, grid=(steps,), in_specs=[smem, smem, vmem,...  8.85 us
    all_to_all x1, starting transfers between devices, body(): lax.all_to_all(early.reshape(owners, hidden // owners, LANES * EARLY), 'd...  8.43 us
  transfers between devices with their start and end apart: 5, of which 4 were waited for; matrix products, arithmetic and copies ran while one was open for 7% of the time, Pallas kernels for 2%

profile of v6, /device:TPU:6, one launch (start us, length us, event | category | flops | bytes accessed | tf_op | source)
XLA Modules:
  0.0 230.9 jit_solution(12511450009023477727)
XLA Ops:
  7.2 0.7 all-gather.3.cloned.1.call-update
  8.6 0.8 copy.32
  9.9 0.7 multiply_add_fusion
  11.9 1.6 pad_maximum_fusion
  13.5 10.4 %all-to-all-start = ((bf16[32,32,1024]{2,1,0:T(8,128)(2,1)}), bf16[32,32,1024]{2,1,0:T(8,128)(2,1)}, u32[]{:S(2)}, u32[]{:S(2)}) async-start(bf16[32,32,1024]{2,1,0:T(8,128)(2,1)} %pad_maximum_fusion), calls=%async_computation | async-start | bytes 4194304 | tf_op jit(solution)/shard_map/all_to_all | solution.py:254
  24.4 25.1 %all-to-all-done = bf16[32,32,1024]{2,1,0:T(8,128)(2,1)} async-done(((bf16[32,32,1024]{2,1,0:T(8,128)(2,1)}), bf16[32,32,1024]{2,1,0:T(8,128)(2,1)}, u32[]{:S(2)}, u32[]{:S(2)}) %all-to-all-start) | async-done | bytes 2097184 | tf_op jit(solution)/shard_map/all_to_all | solution.py:254
  49.5 1.7 fusion.14
  51.8 3.7 %fusion.1.hg_ref = f32[512,768]{1,0:T(8,128)} fusion(bf16[512,1024]{1,0:T(8,128)(2,1)S(1)} %bitcast.41, bf16[1,768,1024]{2,1,0:T(8,128)(2,1)} %param.14, f32[768]{0:T(1024)S(1)} %broadcast_bitcast_fusion), kind=kOutput, calls=%fused_computation.3 | convolution fusion | flops 807665664 | bytes 4197376 | tf_op jit(solution)/shard_map/sd,fd->sf/dot_general | solution.py:263
  55.5 35.0 %all-gather.3.cloned.1.call-done = bf16[1024,1,1536]{2,0,1:T(8,128)(2,1)} async-done(((bf16[64,1,1536]{2,0,1:T(8,128)(2,1)}), bf16[1024,1,1536]{2,0,1:T(8,128)(2,1)}) %all-gather.3.cloned.1.call-update) | async-done | bytes 3145744 | tf_op jit(solution)/shard_map/all_gather | solution.py:241
  90.5 8.9 %shard_map.120 = (bf16[16,1008,128]{2,1,0:T(8,128)(2,1)}, bf16[768,384]{1,0:T(8,128)(2,1)}, bf16[2,512,768]{2,1,0:T(8,128)(2,1)}, f32[512,1]{1,0:T(8,128)}) custom-call(f32[8,2]{1,0:T(8,128)S(1)} %copy.35.gu_scale, f32[6]{0:T(128)S(1)} %select_reduce_fusion.2.d_scale, bf16[512,1024]{1,0:T(8,128)(2,1)S(1)} %bitcast.39, bf16[1024,512]{1,0:T(8,128)(2,1)S(1)} %bitcast.40, ...), custom_call_target="tpu_custom_call" | custom-call | flops 4026531840 | bytes 14680064 | tf_op jit(solution)/shard_map/pallas_call | solution.py:110
  99.4 8.4 %all-to-all-start.1 = ((bf16[16,48,384]{2,1,0:T(8,128)(2,1)}), bf16[16,48,384]{2,1,0:T(8,128)(2,1)}, u32[]{:S(2)}, u32[]{:S(2)}) async-start(bf16[16,48,384]{2,1,0:T(8,128)(2,1)} %bitcast.48), calls=%async_computation.2 | async-start | bytes 1179648 | tf_op jit(solution)/shard_map/all_to_all | solution.py:267
  107.8 1.4 copy-done.3
  109.2 0.9 copy-done.4
  110.2 3.8 %shard_map.121 = bf16[512,1152]{1,0:T(8,128)(2,1)S(1)} custom-call(f32[8,2]{1,0:T(8,128)S(1)} %copy.35.gu_scale, bf16[2,512,768]{2,1,0:T(8,128)(2,1)S(1)} %copy-done.3, f32[512,1]{1,0:T(8,128)S(1)} %copy-done.4, bf16[1024,1536]{1,0:T(8,128)(2,1)S(1)} %bitcast.35, bf16[1024,1536]{1,0:T(8,128)(2,1)S(1)} %bitcast.36), custom_call_target="tpu_custom_call" | custom-call | flops 1610612736 | bytes 6291456 | tf_op jit(solution)/shard_map/pallas_call | solution.py:175
  114.0 1.0 copy-done.2
  115.0 18.0 %all-to-all-done.1 = bf16[16,48,384]{2,1,0:T(8,128)(2,1)} async-done(((bf16[16,48,384]{2,1,0:T(8,128)(2,1)}), bf16[16,48,384]{2,1,0:T(8,128)(2,1)}, u32[]{:S(2)}, u32[]{:S(2)}) %all-to-all-start.1) | async-done | bytes 589856 | tf_op jit(solution)/shard_map/all_to_all | solution.py:267
  133.1 7.3 %all-to-all-start.2 = ((bf16[32,16,1152]{2,1,0:T(8,128)(2,1)}), bf16[32,16,1152]{2,1,0:T(8,128)(2,1)S(1)}, u32[]{:S(2)}, u32[]{:S(2)}) async-start(bf16[32,16,1152]{2,1,0:T(8,128)(2,1)} %bitcast.37), calls=%async_computation.3 | async-start | bytes 2359296 | tf_op jit(solution)/shard_map/all_to_all | solution.py:276
  140.4 1.2 reduce_sum.64
  141.6 38.0 %all_gather.10 = bf16[768,384]{1,0:T(8,128)(2,1)S(1)} all-gather(bf16[48,384]{1,0:T(8,128)(2,1)S(1)} %reduce_sum.64), channel_id=1, replica_groups=mesh['dp'=16,'expert'=32] {'dp'}, dimensions={0}, use_global_device_ids=true | all-gather | bytes 626688 | tf_op jit(solution)/shard_map/all_gather | solution.py:283
  180.5 1.0 convolution_convert_fusion.2
  181.5 6.0 %reduce-scatter.2.cloned.1.call-done = bf16[1,1008,128]{2,1,0:T(8,128)(2,1)} async-done(((bf16[16,1008,128]{2,1,0:T(8,128)(2,1)}), bf16[1,1008,128]{2,1,0:T(8,128)(2,1)}) %reduce-scatter.2.cloned.1.call-update) | async-done | bytes 258064 | tf_op jit(solution)/shard_map/reduce_scatter | solution.py:266
  187.5 1.7 shard_map.122
  189.2 33.5 %all_gather.11 = bf16[3,256,640]{2,1,0:T(8,128)(2,1)S(1)} all-gather(bf16[3,16,640]{2,1,0:T(8,128)(2,1)} %get-tuple-element.27), channel_id=1, replica_groups=mesh['dp'=16,'expert'=32] {'dp'}, dimensions={1}, use_global_device_ids=true | all-gather | bytes 1044480 | tf_op jit(solution)/shard_map/all_gather | solution.py:300
  222.7 1.4 maximum_bitcast_fusion
  (38 shorter events, 4.5 us)
Async XLA Ops:
  7.2 3.8 %copy-start = (bf16[128,1024]{1,0:T(8,128)(2,1)S(1)}, bf16[128,1024]{1,0:T(8,128)(2,1)}, u32[]{:S(2)}) copy-start(bf16[128,1024]{1,0:T(8,128)(2,1)} %param.10) | copy-start | bytes 786436
  7.2 4.2 %copy-start.5 = (bf16[128,1024]{1,0:T(8,128)(2,1)S(1)}, bf16[128,1024]{1,0:T(8,128)(2,1)}, u32[]{:S(2)}) copy-start(bf16[128,1024]{1,0:T(8,128)(2,1)} %param.9) | copy-start | bytes 786436
  7.2 83.3 %all-gather.3.cloned.1.call-start = ((), (), s32[]{:S(2)}) async-start(), calls=%async_computation.5 | async-start | bytes 3342336 | tf_op jit(solution)/shard_map/all_gather | solution.py:241
  13.5 10.4 %copy-start.6 = (s32[8,1,2]{0,2,1:T(2,128)S(1)}, s32[8,1,2]{0,2,1:T(2,128)}, u32[]{:S(2)}) copy-start(s32[8,1,2]{0,2,1:T(2,128)} %param.15) | copy-start | bytes 196
  13.5 10.4 %copy-start.7 = (f32[16]{0:T(128)S(1)}, f32[16]{0:T(128)}, u32[]{:S(2)}) copy-start(f32[16]{0:T(128)} %param.17) | copy-start | bytes 196
  13.5 10.7 %copy-start.9 = (s32[1,6]{1,0:T(1,128)S(1)}, s32[1,6]{1,0:T(1,128)}, u32[]{:S(2)}) copy-start(s32[1,6]{1,0:T(1,128)} %param.16) | copy-start | bytes 76
  13.5 36.0 %all-to-all-start = ((bf16[32,32,1024]{2,1,0:T(8,128)(2,1)}), bf16[32,32,1024]{2,1,0:T(8,128)(2,1)}, u32[]{:S(2)}, u32[]{:S(2)}) async-start(bf16[32,32,1024]{2,1,0:T(8,128)(2,1)} %pad_maximum_fusion), calls=%async_computation | async-start | bytes 4194304 | tf_op jit(solution)/shard_map/all_to_all | solution.py:254
  23.9 163.6 %reduce-scatter.2.cloned.1.call-start = ((), (), s32[]{:S(2)}) async-start(), calls=%async_computation.4 | async-start | bytes 4386816 | tf_op jit(solution)/shard_map/reduce_scatter | solution.py:266
  99.3 8.5 %copy-start.1 = (bf16[1024,1,1536]{2,0,1:T(8,128)(2,1)S(1)}, bf16[1024,1,1536]{2,0,1:T(8,128)(2,1)}, u32[]{:S(2)}) copy-start(bf16[1024,1,1536]{2,0,1:T(8,128)(2,1)} %all-gather.3.cloned.1.call-done) | copy-start | bytes 9437188
  99.4 33.7 %all-to-all-start.1 = ((bf16[16,48,384]{2,1,0:T(8,128)(2,1)}), bf16[16,48,384]{2,1,0:T(8,128)(2,1)}, u32[]{:S(2)}, u32[]{:S(2)}) async-start(bf16[16,48,384]{2,1,0:T(8,128)(2,1)} %bitcast.48), calls=%async_computation.2 | async-start | bytes 1179648 | tf_op jit(solution)/shard_map/all_to_all | solution.py:267
  107.8 1.4 copy-start.3
  109.2 0.9 copy-start.4
  114.0 1.0 copy-start.2
  115.0 64.8 %copy-start.8 = (bf16[128,2]{0,1:T(2,128)(2,1)S(1)}, bf16[128,2]{0,1:T(2,128)(2,1)}, u32[]{:S(2)}) copy-start(bf16[128,2]{0,1:T(2,128)(2,1)} %param.12) | copy-start | bytes 1540
  133.1 46.5 %all-to-all-start.2 = ((bf16[32,16,1152]{2,1,0:T(8,128)(2,1)}), bf16[32,16,1152]{2,1,0:T(8,128)(2,1)S(1)}, u32[]{:S(2)}, u32[]{:S(2)}) async-start(bf16[32,16,1152]{2,1,0:T(8,128)(2,1)} %bitcast.37), calls=%async_computation.3 | async-start | bytes 2359296 | tf_op jit(solution)/shard_map/all_to_all | solution.py:276
Sparse Core Ops, SparseCore 0:
  10.1 80.3 all-gather.2
  99.5 87.9 reduce-scatter.1

commit v7 on v6

--- a/solution.py
+++ b/solution.py
@@ -264,12 +264,24 @@
 
     sums, early, joint, dots = hidden_step(gu_scale, d_scale, x, xt, g, hg, gathered, owners)
     mine = lax.psum_scatter(sums, "dp", scatter_dimension=0, tiled=True)
+    half = hidden // 2
+    parity = lax.axis_index("dp") % 2
+    given = lax.ppermute(
+        lax.dynamic_slice_in_dim(early, (1 - parity) * half, half, axis=0),
+        "dp",
+        [(z, z + 1 - 2 * (z % 2)) for z in range(owners)],
+    )
+    kept = lax.dynamic_slice_in_dim(early, parity * half, half, axis=0)
+    same_parity = [list(range(k, owners, 2)) for k in range(2)]
     parts = lax.all_to_all(
-        early.reshape(owners, hidden // owners, LANES * EARLY),
+        (kept.astype(f32) + given.astype(f32))
+        .astype(bf16)
+        .reshape(owners // 2, hidden // owners, LANES * EARLY),
         "dp",
         split_axis=0,
         concat_axis=0,
         tiled=True,
+        axis_index_groups=same_parity,
     )
     row_grads = rows_step(gu_scale, joint, dots, gathered)
     row_grads, parts = lax.optimization_barrier((row_grads, parts))
@@ -281,7 +293,11 @@
         tiled=True,
     ).reshape(slots, width + LANES)
     down_early = lax.all_gather(
-        jnp.sum(parts.astype(f32), axis=0).astype(bf16), "dp", axis=0, tiled=True
+        jnp.sum(parts.astype(f32), axis=0).astype(bf16),
+        "dp",
+        axis=0,
+        tiled=True,
+        axis_index_groups=[same_parity[0] + same_parity[1]],
     )
     token_grad = jnp.dot(either, back[:, :width], preferred_element_type=f32).astype(bf16)
     picked = jnp.einsum(

time: 232 us -> 238 us (1.026)
  waiting for transfers between devices: 84.8 us -> 77.4 us
  blocking collectives: 71.5 us -> 77.4 us
  starting transfers between devices: 26.2 us -> 30.2 us
    all_to_all x1, waiting for transfers between devices: 18 us -> 11.6 us  [body(): lax.all_to_all((kept.astype(f32) + given.astype(f32)).astype(bf16).reshap...]
    reduce_scatter x1, waiting for transfers between devices: 6 us -> 0.01 us  [body(): mine = lax.psum_scatter(sums, 'dp', scatter_dimension=0, tiled=True)]
    ppermute x0 -> x1, waiting for transfers between devices: none -> 5.04 us  [body(): lax.ppermute(lax.dynamic_slice_in_dim(early, (1 - parity) * half, half, a...]
    ppermute x0 -> x1, starting transfers between devices: none -> 3.87 us  [body(): lax.ppermute(lax.dynamic_slice_in_dim(early, (1 - parity) * half, half, a...]
    all_gather x1, blocking collectives: 38 us -> 41.2 us  [body(): lax.all_gather(jnp.sum(parts.astype(f32), axis=0).astype(bf16), 'dp', axi...]
    all_gather x1, blocking collectives: 33.5 us -> 36.1 us  [body(): lax.all_gather(own, 'dp', axis=1, tiled=True).reshape(hidden, late)]
  transfers between devices with their start and end apart: 5 -> 6, of which waited for: 4 -> 4; matrix products, arithmetic and copies ran while one was open for 7% -> 8% of each run, Pallas kernels for 2% -> 2%
where the time goes in v7:
time: 238 us; the launch traced here: 237 us
  waiting for transfers between devices  77.4 us (33%)
  blocking collectives  77.4 us (33%)
  starting transfers between devices  30.2 us (13%)
  Pallas kernels  14.4 us (6%)
  between operations  14.3 us (6%)
  local copies, waits for them, and re-layouts  8.81 us (4%)
  other arithmetic  8.37 us (4%)
  matrix products  6.15 us (3%)
    all_gather x1, blocking collectives, body(): lax.all_gather(jnp.sum(parts.astype(f32), axis=0).astype(bf16), 'dp', axi...  41.2 us
    all_gather x1, blocking collectives, body(): lax.all_gather(own, 'dp', axis=1, tiled=True).reshape(hidden, late)  36.1 us
    all_gather x1, waiting for transfers between devices, body(): lax.all_gather(gate_up_weight.reshape(gate_up_weight.shape[0], 2 * hidden...  35 us
    all_to_all x1, waiting for transfers between devices, body(): lax.all_to_all(send, 'expert', split_axis=0, concat_axis=0, tiled=True)  25.1 us
    all_to_all x1, waiting for transfers between devices, body(): lax.all_to_all((kept.astype(f32) + given.astype(f32)).astype(bf16).reshap...  11.6 us
    all_to_all x1, starting transfers between devices, body(): lax.all_to_all(send, 'expert', split_axis=0, concat_axis=0, tiled=True)  10.4 us
    pallas_call x1, Pallas kernels, hidden_step(): pl.pallas_call(hidden_kernel, grid=(steps,), in_specs=[smem, smem, vmem,...  8.85 us
    all_to_all x1, starting transfers between devices, body(): lax.all_to_all((kept.astype(f32) + given.astype(f32)).astype(bf16).reshap...  8.01 us
  transfers between devices with their start and end apart: 6, of which 4 were waited for; matrix products, arithmetic and copies ran while one was open for 8% of the time, Pallas kernels for 2%

profile of v7, /device:TPU:6, one launch (start us, length us, event | category | flops | bytes accessed | tf_op | source)
XLA Modules:
  0.0 236.9 jit_solution(12960698315971976604)
XLA Ops:
  11.9 1.6 pad_maximum_fusion
  13.5 10.4 %all-to-all-start = ((bf16[32,32,1024]{2,1,0:T(8,128)(2,1)}), bf16[32,32,1024]{2,1,0:T(8,128)(2,1)}, u32[]{:S(2)}, u32[]{:S(2)}) async-start(bf16[32,32,1024]{2,1,0:T(8,128)(2,1)} %pad_maximum_fusion), calls=%async_computation | async-start | bytes 4194304 | tf_op jit(solution)/shard_map/all_to_all | solution.py:254
  24.4 25.1 %all-to-all-done = bf16[32,32,1024]{2,1,0:T(8,128)(2,1)} async-done(((bf16[32,32,1024]{2,1,0:T(8,128)(2,1)}), bf16[32,32,1024]{2,1,0:T(8,128)(2,1)}, u32[]{:S(2)}, u32[]{:S(2)}) %all-to-all-start) | async-done | bytes 2097184 | tf_op jit(solution)/shard_map/all_to_all | solution.py:254
  49.5 1.7 fusion.14
  51.8 3.7 %fusion.1.hg_ref = f32[512,768]{1,0:T(8,128)} fusion(bf16[512,1024]{1,0:T(8,128)(2,1)S(1)} %bitcast.41, bf16[1,768,1024]{2,1,0:T(8,128)(2,1)} %param.14, f32[768]{0:T(1024)S(1)} %broadcast_bitcast_fusion), kind=kOutput, calls=%fused_computation.3 | convolution fusion | flops 807665664 | bytes 4197376 | tf_op jit(solution)/shard_map/sd,fd->sf/dot_general | solution.py:263
  55.5 35.0 %all-gather.3.cloned.1.call-done = bf16[1024,1,1536]{2,0,1:T(8,128)(2,1)} async-done(((bf16[64,1,1536]{2,0,1:T(8,128)(2,1)}), bf16[1024,1,1536]{2,0,1:T(8,128)(2,1)}) %all-gather.3.cloned.1.call-update) | async-done | bytes 3145744 | tf_op jit(solution)/shard_map/all_gather | solution.py:241
  90.5 8.9 %shard_map.120 = (bf16[16,1008,128]{2,1,0:T(8,128)(2,1)}, bf16[768,384]{1,0:T(8,128)(2,1)}, bf16[2,512,768]{2,1,0:T(8,128)(2,1)}, f32[512,1]{1,0:T(8,128)}) custom-call(f32[8,2]{1,0:T(8,128)S(1)} %copy.35.gu_scale, f32[6]{0:T(128)S(1)} %select_reduce_fusion.2.d_scale, bf16[512,1024]{1,0:T(8,128)(2,1)S(1)} %bitcast.39, bf16[1024,512]{1,0:T(8,128)(2,1)S(1)} %bitcast.40, ...), custom_call_target="tpu_custom_call" | custom-call | flops 4026531840 | bytes 14680064 | tf_op jit(solution)/shard_map/pallas_call | solution.py:110
  99.4 1.9 constant_dynamic-slice_fusion
  101.2 3.9 %collective-permute-start = (bf16[384,384]{1,0:T(8,128)(2,1)}, bf16[384,384]{1,0:T(8,128)(2,1)}, u32[]{:S(2)}, u32[]{:S(2)}) collective-permute-start(bf16[384,384]{1,0:T(8,128)(2,1)} %constant_dynamic-slice_fusion), channel_id=1, source_target_pairs={{0,32},{32,0},{64,96},{96,64},{128,160},{160,128},{192,224},{224,1... | collective-permute-start | bytes 884744 | tf_op jit(solution)/shard_map/ppermute | solution.py:269
  105.1 5.0 %collective-permute-done = bf16[384,384]{1,0:T(8,128)(2,1)} collective-permute-done((bf16[384,384]{1,0:T(8,128)(2,1)}, bf16[384,384]{1,0:T(8,128)(2,1)}, u32[]{:S(2)}, u32[]{:S(2)}) %collective-permute-start) | collective-permute-done | bytes 294944 | tf_op jit(solution)/shard_map/ppermute | solution.py:269
  110.2 1.8 add_convert_fusion
  112.0 8.0 %all-to-all-start.1 = ((bf16[8,48,384]{2,1,0:T(8,128)(2,1)}), bf16[8,48,384]{2,1,0:T(8,128)(2,1)}, u32[]{:S(2)}, u32[]{:S(2)}) async-start(bf16[8,48,384]{2,1,0:T(8,128)(2,1)} %bitcast.46), calls=%async_computation.2 | async-start | bytes 589824 | tf_op jit(solution)/shard_map/all_to_all | solution.py:276
  120.0 1.4 copy-done.3
  121.4 1.0 copy-done.4
  122.4 3.8 %shard_map.121 = bf16[512,1152]{1,0:T(8,128)(2,1)S(1)} custom-call(f32[8,2]{1,0:T(8,128)S(1)} %copy.35.gu_scale, bf16[2,512,768]{2,1,0:T(8,128)(2,1)S(1)} %copy-done.3, f32[512,1]{1,0:T(8,128)S(1)} %copy-done.4, bf16[1024,1536]{1,0:T(8,128)(2,1)S(1)} %bitcast.35, bf16[1024,1536]{1,0:T(8,128)(2,1)S(1)} %bitcast.36), custom_call_target="tpu_custom_call" | custom-call | flops 1610612736 | bytes 6291456 | tf_op jit(solution)/shard_map/pallas_call | solution.py:175
  126.2 1.0 copy-done.2
  127.3 11.6 %all-to-all-done.1 = bf16[8,48,384]{2,1,0:T(8,128)(2,1)} async-done(((bf16[8,48,384]{2,1,0:T(8,128)(2,1)}), bf16[8,48,384]{2,1,0:T(8,128)(2,1)}, u32[]{:S(2)}, u32[]{:S(2)}) %all-to-all-start.1) | async-done | bytes 294944 | tf_op jit(solution)/shard_map/all_to_all | solution.py:276
  138.8 7.9 %all-to-all-start.2 = ((bf16[32,16,1152]{2,1,0:T(8,128)(2,1)}), bf16[32,16,1152]{2,1,0:T(8,128)(2,1)S(1)}, u32[]{:S(2)}, u32[]{:S(2)}) async-start(bf16[32,16,1152]{2,1,0:T(8,128)(2,1)} %bitcast.37), calls=%async_computation.3 | async-start | bytes 2359296 | tf_op jit(solution)/shard_map/all_to_all | solution.py:288
  146.7 1.0 reduce_sum.64
  147.7 41.2 %all_gather.10 = bf16[768,384]{1,0:T(8,128)(2,1)S(1)} all-gather(bf16[48,384]{1,0:T(8,128)(2,1)S(1)} %reduce_sum.64), channel_id=1, replica_groups={{0,64,128,192,256,320,384,448,32,96,160,224,288,352,416,480},{1,65,129,..., dimensions={0}, use_global_device_ids=true | all-gather | bytes 626688 | tf_op jit(solution)/shard_map/all_gather | solution.py:295
  189.9 1.0 convolution_convert_fusion.2
  190.9 1.7 shard_map.122
  192.6 36.1 %all_gather.11 = bf16[3,256,640]{2,1,0:T(8,128)(2,1)S(1)} all-gather(bf16[3,16,640]{2,1,0:T(8,128)(2,1)} %get-tuple-element.27), channel_id=1, replica_groups=mesh['dp'=16,'expert'=32] {'dp'}, dimensions={1}, use_global_device_ids=true | all-gather | bytes 1044480 | tf_op jit(solution)/shard_map/all_gather | solution.py:316
  228.7 1.4 maximum_bitcast_fusion
  (42 shorter events, 6.6 us)
Async XLA Ops:
  7.2 3.8 %copy-start = (bf16[128,1024]{1,0:T(8,128)(2,1)S(1)}, bf16[128,1024]{1,0:T(8,128)(2,1)}, u32[]{:S(2)}) copy-start(bf16[128,1024]{1,0:T(8,128)(2,1)} %param.10) | copy-start | bytes 786436
  7.2 4.2 %copy-start.5 = (bf16[128,1024]{1,0:T(8,128)(2,1)S(1)}, bf16[128,1024]{1,0:T(8,128)(2,1)}, u32[]{:S(2)}) copy-start(bf16[128,1024]{1,0:T(8,128)(2,1)} %param.9) | copy-start | bytes 786436
  7.2 83.3 %all-gather.3.cloned.1.call-start = ((), (), s32[]{:S(2)}) async-start(), calls=%async_computation.5 | async-start | bytes 3342336 | tf_op jit(solution)/shard_map/all_gather | solution.py:241
  13.5 10.4 %copy-start.6 = (s32[8,1,2]{0,2,1:T(2,128)S(1)}, s32[8,1,2]{0,2,1:T(2,128)}, u32[]{:S(2)}) copy-start(s32[8,1,2]{0,2,1:T(2,128)} %param.15) | copy-start | bytes 196
  13.5 10.4 %copy-start.7 = (f32[16]{0:T(128)S(1)}, f32[16]{0:T(128)}, u32[]{:S(2)}) copy-start(f32[16]{0:T(128)} %param.17) | copy-start | bytes 196
  13.5 10.7 %copy-start.9 = (s32[1,6]{1,0:T(1,128)S(1)}, s32[1,6]{1,0:T(1,128)}, u32[]{:S(2)}) copy-start(s32[1,6]{1,0:T(1,128)} %param.16) | copy-start | bytes 76
  13.5 36.0 %all-to-all-start = ((bf16[32,32,1024]{2,1,0:T(8,128)(2,1)}), bf16[32,32,1024]{2,1,0:T(8,128)(2,1)}, u32[]{:S(2)}, u32[]{:S(2)}) async-start(bf16[32,32,1024]{2,1,0:T(8,128)(2,1)} %pad_maximum_fusion), calls=%async_computation | async-start | bytes 4194304 | tf_op jit(solution)/shard_map/all_to_all | solution.py:254
  23.8 167.1 %reduce-scatter.2.cloned.1.call-start = ((), (), s32[]{:S(2)}) async-start(), calls=%async_computation.4 | async-start | bytes 4386816 | tf_op jit(solution)/shard_map/reduce_scatter | solution.py:266
  99.3 20.7 %copy-start.1 = (bf16[1024,1,1536]{2,0,1:T(8,128)(2,1)S(1)}, bf16[1024,1,1536]{2,0,1:T(8,128)(2,1)}, u32[]{:S(2)}) copy-start(bf16[1024,1,1536]{2,0,1:T(8,128)(2,1)} %all-gather.3.cloned.1.call-done) | copy-start | bytes 9437188
  101.2 8.9 %collective-permute-start = (bf16[384,384]{1,0:T(8,128)(2,1)}, bf16[384,384]{1,0:T(8,128)(2,1)}, u32[]{:S(2)}, u32[]{:S(2)}) collective-permute-start(bf16[384,384]{1,0:T(8,128)(2,1)} %constant_dynamic-slice_fusion), channel_id=1, source_target_pairs={{0,32},{32,0},{64,96},{96,64},{128,160},{160,128},{192,224},{224,1... | collective-permute-start | bytes 884744 | tf_op jit(solution)/shard_map/ppermute | solution.py:269
  112.0 26.8 %all-to-all-start.1 = ((bf16[8,48,384]{2,1,0:T(8,128)(2,1)}), bf16[8,48,384]{2,1,0:T(8,128)(2,1)}, u32[]{:S(2)}, u32[]{:S(2)}) async-start(bf16[8,48,384]{2,1,0:T(8,128)(2,1)} %bitcast.46), calls=%async_computation.2 | async-start | bytes 589824 | tf_op jit(solution)/shard_map/all_to_all | solution.py:276
  120.0 1.4 copy-start.3
  121.4 1.0 copy-start.4
  126.2 1.0 copy-start.2
  127.2 62.0 %copy-start.8 = (bf16[128,2]{0,1:T(2,128)(2,1)S(1)}, bf16[128,2]{0,1:T(2,128)(2,1)}, u32[]{:S(2)}) copy-start(bf16[128,2]{0,1:T(2,128)(2,1)} %param.12) | copy-start | bytes 1540
  138.8 50.1 %all-to-all-start.2 = ((bf16[32,16,1152]{2,1,0:T(8,128)(2,1)}), bf16[32,16,1152]{2,1,0:T(8,128)(2,1)S(1)}, u32[]{:S(2)}, u32[]{:S(2)}) async-start(bf16[32,16,1152]{2,1,0:T(8,128)(2,1)} %bitcast.37), calls=%async_computation.3 | async-start | bytes 2359296 | tf_op jit(solution)/shard_map/all_to_all | solution.py:288
Sparse Core Ops, SparseCore 0:
  10.1 80.3 all-gather.2
  99.5 89.6 reduce-scatter.1
